TPU v7x, 256 devices: a whole 4x4x8 slice. The times are simulated.
256 devices in a mesh: gx: 8 (over y, core), gy: 8 (over z_hi, x), af: 4 (over z_lo).
Axes of the slice: x: 4, y: 4, z: 8 (z_hi: 2, z_lo: 4; z = z_hi * 4 + z_lo), core: 2. Of those that a mesh axis runs over, the one named last changes fastest.
Arguments:
- volume: bfloat16 [32, 32, 128, 128], P('af', 'gx', 'gy'), may hold values from -6 to 6
- weight_one: bfloat16 [32, 32, 3, 3, 3], P('af'), may hold values from -0.21875 to 0.21875
- bias_one: float32 [32], P('af'), may hold values from -1 to 1
- weight_two: bfloat16 [32, 32, 3, 3, 3], P('af'), may hold values from -0.21875 to 0.21875
- cotangent: bfloat16 [32, 32, 128, 128], P('af', 'gx', 'gy'), may hold values from -6 to 6
Outputs:
- output: bfloat16 [32, 32, 128, 128], P('af', 'gx', 'gy')
- input_grad: bfloat16 [32, 32, 128, 128], P('af', 'gx', 'gy')
- grad_one: float32 [32, 32, 3, 3, 3], P('af')
- bias_grad: float32 [32], P('af')
- grad_two: float32 [32, 32, 3, 3, 3], P('af')
All inputs are finite; a program needn't handle non-finite values.
Results may differ from a plain program's by a relative error of at most 0.0065.
Values may be sent and summed in bfloat16 or wider, within the bound.
A program may use at most 64 MiB of HBM per device.

v0:
```python
import math

import jax
import jax.numpy as jnp
from jax import lax
from jax.sharding import PartitionSpec as P


def with_halo(cells, sides, width):
    for axis, dim in sides:
        count = lax.axis_size(axis)
        ends = count - 1
        head = lax.slice_in_dim(cells, 0, width, axis=dim)
        tail = lax.slice_in_dim(cells, cells.shape[dim] - width, cells.shape[dim], axis=dim)
        cells = jnp.concatenate(
            [
                lax.ppermute(tail, axis, [(i, (i + 1) % count) for i in range(ends)]),
                cells,
                lax.ppermute(head, axis, [((i + 1) % count, i) for i in range(ends)]),
            ],
            axis=dim,
        )
    return cells


def conv_valid(padded, weight):
    size_x = padded.shape[1] - 2
    size_y = padded.shape[2] - 2
    size_z = padded.shape[3] - 2
    total = jnp.zeros((weight.shape[0], size_x, size_y, size_z), jnp.float32)
    for off_x in range(3):
        for off_y in range(3):
            for off_z in range(3):
                window = padded[
                    :, off_x : off_x + size_x, off_y : off_y + size_y, off_z : off_z + size_z
                ]
                total = total + jnp.einsum(
                    "oi,ixyz->oxyz",
                    weight[:, :, off_x, off_y, off_z],
                    window,
                    preferred_element_type=jnp.float32,
                )
    return total


def kernel_grad(padded, cot_field):
    size_x = cot_field.shape[1]
    size_y = cot_field.shape[2]
    size_z = cot_field.shape[3]
    blocks = []
    for off_x in range(3):
        for off_y in range(3):
            for off_z in range(3):
                window = padded[
                    :, off_x : off_x + size_x, off_y : off_y + size_y, off_z : off_z + size_z
                ]
                blocks.append(
                    jnp.einsum(
                        "oxyz,ixyz->oi", cot_field, window, preferred_element_type=jnp.float32
                    )
                )
    stacked = jnp.stack(blocks, axis=-1)
    return stacked.reshape(cot_field.shape[0], padded.shape[0], 3, 3, 3)


def flipped(weight):
    return jnp.transpose(jnp.flip(weight, (2, 3, 4)), (1, 0, 2, 3, 4))


def depth_pad(values):
    return jnp.pad(values, ((0, 0), (0, 0), (0, 0), (1, 1)))


def full_padded(values):
    gathered = lax.all_gather(values, "af", axis=0, tiled=True)
    rimmed = with_halo(gathered, (("gx", 1), ("gy", 2)), 1)
    return depth_pad(rimmed)


def silu_grad(hidden_grad, pre_act):
    sigma_vals = jax.nn.sigmoid(pre_act)
    return (hidden_grad * sigma_vals * (1.0 + pre_act * (1.0 - sigma_vals))).astype(jnp.bfloat16)


def body(volume, weight_one, bias_one, weight_two, cotangent):
    own_rows = volume.shape[0]
    vol_pad = full_padded(volume)
    pre_act = conv_valid(vol_pad, weight_one) + bias_one[:, None, None, None]
    hidden = jax.nn.silu(pre_act).astype(jnp.bfloat16)
    hid_pad = full_padded(hidden)
    output = conv_valid(hid_pad, weight_two).astype(jnp.bfloat16)
    local_two = kernel_grad(hid_pad, cotangent)
    every_one, every_two = (
        lax.all_gather(weight_one, "af", axis=0, tiled=True),
        lax.all_gather(weight_two, "af", axis=0, tiled=True),
    )
    first_row = lax.axis_index("af") * own_rows

    def transposed(cot_field, every_w):
        padded = full_padded(cot_field)
        turned = lax.dynamic_slice_in_dim(flipped(every_w), first_row, own_rows, 0)
        return conv_valid(padded, turned)

    hidden_grad = transposed(cotangent, every_two)
    pre_grad = silu_grad(hidden_grad, pre_act)
    local_one = kernel_grad(vol_pad, pre_grad)
    local_bias = jnp.sum(pre_grad, axis=(1, 2, 3), dtype=jnp.float32)
    input_grad = transposed(pre_grad, every_one).astype(jnp.bfloat16)
    summed_one, summed_bias, summed_two = lax.psum((local_one, local_bias, local_two), ("gx", "gy"))
    cell_total = (
        volume.shape[1]
        * lax.axis_size("gx")
        * volume.shape[2]
        * lax.axis_size("gy")
        * volume.shape[3]
    )
    grad_scale = 1.0 / math.sqrt(cell_total)
    return (
        output,
        input_grad,
        summed_one * grad_scale,
        summed_bias * grad_scale,
        summed_two * grad_scale,
    )


def solution(mesh):
    return jax.shard_map(
        body,
        mesh=mesh,
        in_specs=(
            P("af", "gx", "gy", None),
            P("af", None, None, None, None),
            P("af"),
            P("af", None, None, None, None),
            P("af", "gx", "gy", None),
        ),
        out_specs=(
            P("af", "gx", "gy", None),
            P("af", "gx", "gy", None),
            P("af", None, None, None, None),
            P("af"),
            P("af", None, None, None, None),
        ),
        check_vma=False,
    )
```

profile of v0, /device:TPU:0, one launch (start us, length us, event | category | flops | bytes accessed | tf_op | source)
XLA Modules:
  0.0 645.6 jit_solution(11498958030644135914)
XLA Ops:
  1.7 14.6 %all_gather.18 = bf16[32,4,16,128]{3,0,2,1:T(8,128)(2,1)S(1)} all-gather(bf16[8,4,16,128]{3,0,2,1:T(8,128)(2,1)S(1)} %copy.43), channel_id=1, replica_groups=mesh['gx'=8,'gy'=8,'af'=4] {'af'}, dimensions={0}, use_global_device_ids=true | all-gather | bytes 655360 | tf_op jit(solution)/shard_map/all_gather | solution.py:75
  16.3 1.3 collective-permute-start
  17.6 1.3 collective-permute-start.1
  19.9 15.3 %all_gather.22 = bf16[32,4,16,128]{3,0,2,1:T(8,128)(2,1)S(1)} all-gather(bf16[8,4,16,128]{3,0,2,1:T(8,128)(2,1)S(1)} %copy.46), channel_id=1, replica_groups=mesh['gx'=8,'gy'=8,'af'=4] {'af'}, dimensions={0}, use_global_device_ids=true | all-gather | bytes 655360 | tf_op jit(solution)/shard_map/all_gather | solution.py:75
  35.2 2.1 collective-permute-start.8
  37.4 1.3 collective-permute-start.9
  38.9 13.0 %all_gather.21 = bf16[32,32,3,3,3]{1,0,4,3,2:T(8,128)(2,1)S(1)} all-gather(bf16[8,32,3,3,3]{1,0,4,3,2:T(8,128)(2,1)S(1)} %copy-done.48), channel_id=1, replica_groups=mesh['gx'=8,'gy'=8,'af'=4] {'af'}, dimensions={0}, use_global_device_ids=true | all-gather | bytes 69120 | tf_op jit(solution)/shard_map/all_gather | solution.py:95
  52.3 13.0 %all_gather.20 = bf16[32,32,3,3,3]{1,0,4,3,2:T(8,128)(2,1)S(1)} all-gather(bf16[8,32,3,3,3]{1,0,4,3,2:T(8,128)(2,1)S(1)} %copy-done.50), channel_id=1, replica_groups=mesh['gx'=8,'gy'=8,'af'=4] {'af'}, dimensions={0}, use_global_device_ids=true | all-gather | bytes 69120 | tf_op jit(solution)/shard_map/all_gather | solution.py:94
  66.0 3.4 collective-permute-start.2
  69.4 1.3 collective-permute-start.3
  71.2 4.5 collective-permute-start.10
  75.8 1.5 collective-permute-start.11
  92.0 15.4 %all_gather.23 = bf16[32,4,16,128]{3,0,2,1:T(8,128)(2,1)S(1)} all-gather(bf16[8,4,16,128]{3,0,2,1:T(8,128)(2,1)S(1)} %get-tuple-element.51), channel_id=1, replica_groups=mesh['gx'=8,'gy'=8,'af'=4] {'af'}, dimensions={0}, use_global_device_ids=true | all-gather | bytes 655360 | tf_op jit(solution)/shard_map/all_gather | solution.py:75
  107.4 14.4 %all_gather.19 = bf16[32,4,16,128]{3,0,2,1:T(8,128)(2,1)S(1)} all-gather(bf16[8,4,16,128]{3,0,2,1:T(8,128)(2,1)S(1)} %get-tuple-element.48), channel_id=1, replica_groups=mesh['gx'=8,'gy'=8,'af'=4] {'af'}, dimensions={0}, use_global_device_ids=true | all-gather | bytes 655360 | tf_op jit(solution)/shard_map/all_gather | solution.py:75
  122.7 1.3 collective-permute-start.4
  123.9 1.5 collective-permute-start.5
  132.2 8.9 %collective-permute-start.12 = (bf16[32,1,16,128]{3,0,2,1:T(8,128)(2,1)S(1)}, bf16[32,1,16,128]{3,0,2,1:T(8,128)(2,1)S(1)}, u32[]{:S(2)}, u32[]{:S(2)}) collective-permute-start(bf16[32,1,16,128]{3,0,2,1:T(8,128)(2,1)S(1)} %get-tuple-element.27), channel_id=1, source_target_pairs={{0,32},{32,64},{64,96},{96,128},{128,160},{160,192},{192,224},{1,3... | collective-permute-start | bytes 393224 | tf_op jit(solution)/shard_map/ppermute | solution.py:17
  141.1 1.3 collective-permute-start.13
  144.3 4.4 collective-permute-start.6
  148.7 1.3 collective-permute-start.7
  150.2 9.7 %collective-permute-start.14 = (bf16[32,6,1,128]{3,0,2,1:T(8,128)(2,1)S(1)}, bf16[32,6,1,128]{3,0,2,1:T(8,128)(2,1)S(1)}, u32[]{:S(2)}, u32[]{:S(2)}) collective-permute-start(bf16[32,6,1,128]{3,0,2,1:T(8,128)(2,1)S(1)} %get-tuple-element.18), channel_id=1, source_target_pairs={{0,4},{4,8},{8,12},{12,16},{16,20},{20,24},{24,28},{1,5},{5,9},{9,... | collective-permute-start | bytes 147464 | tf_op jit(solution)/shard_map/ppermute | solution.py:17
  160.0 1.3 collective-permute-start.15
  164.8 7.0 %collective-permute-done.15 = bf16[32,6,1,128]{3,0,2,1:T(8,128)(2,1)S(1)} collective-permute-done((bf16[32,6,1,128]{3,0,2,1:T(8,128)(2,1)S(1)}, bf16[32,6,1,128]{3,0,2,1:T(8,128)(2,1)S(1)}, u32[]{:S(2)}, u32[]{:S(2)}) %collective-permute-start.15) | collective-permute-done | bytes 49184 | tf_op jit(solution)/shard_map/ppermute | solution.py:19
  192.3 1.1 fusion.316
  196.1 1.1 fusion.328
  198.1 1.1 convolution_bitcast_fusion.11
  203.0 1.1 convolution_bitcast_fusion.9
  213.4 413.0 %all-reduce.4 = (f32[8,32,3,3,3]{1,0,4,3,2:T(8,128)}, f32[8]{0:T(128)S(1)}, f32[8,32,3,3,3]{1,0,4,3,2:T(8,128)}) all-reduce(f32[8,32,3,3,3]{1,0,4,3,2:T(8,128)} %bitcast.1393, f32[8]{0:T(128)S(1)} %get-tuple-element.50, f32[8,32,3,3,3]{1,0,4,3,2:T(8,128)} %bitcast.1394), channel_id=1, replica_groups=mesh['gx'=8,'gy'=8,'af'=4] {'gx','gy'}, use_global_device_ids=true, to_apply=%region_0.1 | all-reduce | flops 13832 | bytes 110656 | tf_op jit(solution)/shard_map/psum | solution.py:109
  627.0 1.4 fusion.187
  628.3 1.2 fusion.181
  634.5 1.1 fusion.108
  643.1 1.1 fusion.109
  (325 shorter events, 82.6 us)
Async XLA Ops:
  0.6 38.1 %copy-start.50 = (bf16[8,32,3,3,3]{1,0,4,3,2:T(8,128)(2,1)S(1)}, bf16[8,32,3,3,3]{1,0,4,3,2:T(8,128)(2,1)}, u32[]{:S(2)}) copy-start(bf16[8,32,3,3,3]{1,0,4,3,2:T(8,128)(2,1)} %param.6) | copy-start | bytes 41476
  1.7 37.2 %copy-start.48 = (bf16[8,32,3,3,3]{1,0,4,3,2:T(8,128)(2,1)S(1)}, bf16[8,32,3,3,3]{1,0,4,3,2:T(8,128)(2,1)}, u32[]{:S(2)}) copy-start(bf16[8,32,3,3,3]{1,0,4,3,2:T(8,128)(2,1)} %param.8) | copy-start | bytes 41476
  16.3 49.2 %collective-permute-start = (bf16[32,1,16,128]{3,0,2,1:T(8,128)(2,1)S(1)}, bf16[32,1,16,128]{3,0,2,1:T(8,128)(2,1)S(1)}, u32[]{:S(2)}, u32[]{:S(2)}) collective-permute-start(bf16[32,1,16,128]{3,0,2,1:T(8,128)(2,1)S(1)} %get-tuple-element.39), channel_id=1, source_target_pairs={{0,32},{32,64},{64,96},{96,128},{128,160},{160,192},{192,224},{1,3... | collective-permute-start | bytes 393224 | tf_op jit(solution)/shard_map/ppermute | solution.py:17
  17.6 48.3 %collective-permute-start.1 = (bf16[32,1,16,128]{3,0,2,1:T(8,128)(2,1)S(1)}, bf16[32,1,16,128]{3,0,2,1:T(8,128)(2,1)S(1)}, u32[]{:S(2)}, u32[]{:S(2)}) collective-permute-start(bf16[32,1,16,128]{3,0,2,1:T(8,128)(2,1)S(1)} %get-tuple-element.38), channel_id=1, source_target_pairs={{32,0},{64,32},{96,64},{128,96},{160,128},{192,160},{224,192},{33,... | collective-permute-start | bytes 393224 | tf_op jit(solution)/shard_map/ppermute | solution.py:19
  35.2 35.8 %collective-permute-start.8 = (bf16[32,1,16,128]{3,0,2,1:T(8,128)(2,1)S(1)}, bf16[32,1,16,128]{3,0,2,1:T(8,128)(2,1)S(1)}, u32[]{:S(2)}, u32[]{:S(2)}) collective-permute-start(bf16[32,1,16,128]{3,0,2,1:T(8,128)(2,1)S(1)} %get-tuple-element.29), channel_id=1, source_target_pairs={{0,32},{32,64},{64,96},{96,128},{128,160},{160,192},{192,224},{1,3... | collective-permute-start | bytes 393224 | tf_op jit(solution)/shard_map/ppermute | solution.py:17
  37.4 33.8 %collective-permute-start.9 = (bf16[32,1,16,128]{3,0,2,1:T(8,128)(2,1)S(1)}, bf16[32,1,16,128]{3,0,2,1:T(8,128)(2,1)S(1)}, u32[]{:S(2)}, u32[]{:S(2)}) collective-permute-start(bf16[32,1,16,128]{3,0,2,1:T(8,128)(2,1)S(1)} %get-tuple-element.28), channel_id=1, source_target_pairs={{32,0},{64,32},{96,64},{128,96},{160,128},{192,160},{224,192},{33,... | collective-permute-start | bytes 393224 | tf_op jit(solution)/shard_map/ppermute | solution.py:19
  65.5 121.7 %copy-start.47 = (bf16[8,32,3,3,3]{1,0,4,3,2:T(8,128)(2,1)}, bf16[8,32,3,3,3]{1,0,4,3,2:T(8,128)(2,1)S(1)}, u32[]{:S(2)}) copy-start(bf16[8,32,3,3,3]{1,0,4,3,2:T(8,128)(2,1)S(1)} %dynamic-slice_bitcast_fusion.1) | copy-start | bytes 41476
  66.0 11.6 %collective-permute-start.2 = (bf16[32,6,1,128]{3,0,2,1:T(8,128)(2,1)S(1)}, bf16[32,6,1,128]{3,0,2,1:T(8,128)(2,1)S(1)}, u32[]{:S(2)}, u32[]{:S(2)}) collective-permute-start(bf16[32,6,1,128]{3,0,2,1:T(8,128)(2,1)S(1)} %get-tuple-element.24), channel_id=1, source_target_pairs={{0,4},{4,8},{8,12},{12,16},{16,20},{20,24},{24,28},{1,5},{5,9},{9,... | collective-permute-start | bytes 147464 | tf_op jit(solution)/shard_map/ppermute | solution.py:17
  69.4 8.3 %collective-permute-start.3 = (bf16[32,6,1,128]{3,0,2,1:T(8,128)(2,1)S(1)}, bf16[32,6,1,128]{3,0,2,1:T(8,128)(2,1)S(1)}, u32[]{:S(2)}, u32[]{:S(2)}) collective-permute-start(bf16[32,6,1,128]{3,0,2,1:T(8,128)(2,1)S(1)} %get-tuple-element.25), channel_id=1, source_target_pairs={{4,0},{8,4},{12,8},{16,12},{20,16},{24,20},{28,24},{5,1},{9,5},{13... | collective-permute-start | bytes 147464 | tf_op jit(solution)/shard_map/ppermute | solution.py:19
  71.2 11.8 %collective-permute-start.10 = (bf16[32,6,1,128]{3,0,2,1:T(8,128)(2,1)S(1)}, bf16[32,6,1,128]{3,0,2,1:T(8,128)(2,1)S(1)}, u32[]{:S(2)}, u32[]{:S(2)}) collective-permute-start(bf16[32,6,1,128]{3,0,2,1:T(8,128)(2,1)S(1)} %get-tuple-element.20), channel_id=1, source_target_pairs={{0,4},{4,8},{8,12},{12,16},{16,20},{20,24},{24,28},{1,5},{5,9},{9,... | collective-permute-start | bytes 147464 | tf_op jit(solution)/shard_map/ppermute | solution.py:17
  75.8 7.3 %collective-permute-start.11 = (bf16[32,6,1,128]{3,0,2,1:T(8,128)(2,1)S(1)}, bf16[32,6,1,128]{3,0,2,1:T(8,128)(2,1)S(1)}, u32[]{:S(2)}, u32[]{:S(2)}) collective-permute-start(bf16[32,6,1,128]{3,0,2,1:T(8,128)(2,1)S(1)} %get-tuple-element.21), channel_id=1, source_target_pairs={{4,0},{8,4},{12,8},{16,12},{20,16},{24,20},{28,24},{5,1},{9,5},{13... | collective-permute-start | bytes 147464 | tf_op jit(solution)/shard_map/ppermute | solution.py:19
  122.7 21.2 %collective-permute-start.4 = (bf16[32,1,16,128]{3,0,2,1:T(8,128)(2,1)S(1)}, bf16[32,1,16,128]{3,0,2,1:T(8,128)(2,1)S(1)}, u32[]{:S(2)}, u32[]{:S(2)}) collective-permute-start(bf16[32,1,16,128]{3,0,2,1:T(8,128)(2,1)S(1)} %get-tuple-element.34), channel_id=1, source_target_pairs={{0,32},{32,64},{64,96},{96,128},{128,160},{160,192},{192,224},{1,3... | collective-permute-start | bytes 393224 | tf_op jit(solution)/shard_map/ppermute | solution.py:17
  123.9 20.3 %collective-permute-start.5 = (bf16[32,1,16,128]{3,0,2,1:T(8,128)(2,1)S(1)}, bf16[32,1,16,128]{3,0,2,1:T(8,128)(2,1)S(1)}, u32[]{:S(2)}, u32[]{:S(2)}) collective-permute-start(bf16[32,1,16,128]{3,0,2,1:T(8,128)(2,1)S(1)} %get-tuple-element.33), channel_id=1, source_target_pairs={{32,0},{64,32},{96,64},{128,96},{160,128},{192,160},{224,192},{33,... | collective-permute-start | bytes 393224 | tf_op jit(solution)/shard_map/ppermute | solution.py:19
  132.2 17.8 %collective-permute-start.12 = (bf16[32,1,16,128]{3,0,2,1:T(8,128)(2,1)S(1)}, bf16[32,1,16,128]{3,0,2,1:T(8,128)(2,1)S(1)}, u32[]{:S(2)}, u32[]{:S(2)}) collective-permute-start(bf16[32,1,16,128]{3,0,2,1:T(8,128)(2,1)S(1)} %get-tuple-element.27), channel_id=1, source_target_pairs={{0,32},{32,64},{64,96},{96,128},{128,160},{160,192},{192,224},{1,3... | collective-permute-start | bytes 393224 | tf_op jit(solution)/shard_map/ppermute | solution.py:17
  141.1 9.1 %collective-permute-start.13 = (bf16[32,1,16,128]{3,0,2,1:T(8,128)(2,1)S(1)}, bf16[32,1,16,128]{3,0,2,1:T(8,128)(2,1)S(1)}, u32[]{:S(2)}, u32[]{:S(2)}) collective-permute-start(bf16[32,1,16,128]{3,0,2,1:T(8,128)(2,1)S(1)} %get-tuple-element.26), channel_id=1, source_target_pairs={{32,0},{64,32},{96,64},{128,96},{160,128},{192,160},{224,192},{33,... | collective-permute-start | bytes 393224 | tf_op jit(solution)/shard_map/ppermute | solution.py:19
  143.8 6.3 copy-start.51
  144.3 67.9 %copy-start.3 = (bf16[32,6,16,128]{3,0,2,1:T(8,128)(2,1)}, bf16[32,6,16,128]{3,0,2,1:T(8,128)(2,1)S(1)}, u32[]{:S(2)}) copy-start(bf16[32,6,16,128]{3,0,2,1:T(8,128)(2,1)S(1)} %get-tuple-element.43) | copy-start | bytes 2359300
  144.3 43.9 %collective-permute-start.6 = (bf16[32,6,1,128]{3,0,2,1:T(8,128)(2,1)S(1)}, bf16[32,6,1,128]{3,0,2,1:T(8,128)(2,1)S(1)}, u32[]{:S(2)}, u32[]{:S(2)}) collective-permute-start(bf16[32,6,1,128]{3,0,2,1:T(8,128)(2,1)S(1)} %get-tuple-element.22), channel_id=1, source_target_pairs={{0,4},{4,8},{8,12},{12,16},{16,20},{20,24},{24,28},{1,5},{5,9},{9,... | collective-permute-start | bytes 147464 | tf_op jit(solution)/shard_map/ppermute | solution.py:17
  148.7 39.5 %collective-permute-start.7 = (bf16[32,6,1,128]{3,0,2,1:T(8,128)(2,1)S(1)}, bf16[32,6,1,128]{3,0,2,1:T(8,128)(2,1)S(1)}, u32[]{:S(2)}, u32[]{:S(2)}) collective-permute-start(bf16[32,6,1,128]{3,0,2,1:T(8,128)(2,1)S(1)} %get-tuple-element.23), channel_id=1, source_target_pairs={{4,0},{8,4},{12,8},{16,12},{20,16},{24,20},{28,24},{5,1},{9,5},{13... | collective-permute-start | bytes 147464 | tf_op jit(solution)/shard_map/ppermute | solution.py:19
  150.2 21.7 %copy-start = (bf16[32,6,16,128]{3,0,2,1:T(8,128)(2,1)}, bf16[32,6,16,128]{3,0,2,1:T(8,128)(2,1)S(1)}, u32[]{:S(2)}) copy-start(bf16[32,6,16,128]{3,0,2,1:T(8,128)(2,1)S(1)} %constant_dynamic-update-slice_fusion.17) | copy-start | bytes 2359300
  150.2 14.6 %collective-permute-start.14 = (bf16[32,6,1,128]{3,0,2,1:T(8,128)(2,1)S(1)}, bf16[32,6,1,128]{3,0,2,1:T(8,128)(2,1)S(1)}, u32[]{:S(2)}, u32[]{:S(2)}) collective-permute-start(bf16[32,6,1,128]{3,0,2,1:T(8,128)(2,1)S(1)} %get-tuple-element.18), channel_id=1, source_target_pairs={{0,4},{4,8},{8,12},{12,16},{16,20},{20,24},{24,28},{1,5},{5,9},{9,... | collective-permute-start | bytes 147464 | tf_op jit(solution)/shard_map/ppermute | solution.py:17
  160.0 11.9 %collective-permute-start.15 = (bf16[32,6,1,128]{3,0,2,1:T(8,128)(2,1)S(1)}, bf16[32,6,1,128]{3,0,2,1:T(8,128)(2,1)S(1)}, u32[]{:S(2)}, u32[]{:S(2)}) collective-permute-start(bf16[32,6,1,128]{3,0,2,1:T(8,128)(2,1)S(1)} %get-tuple-element.19), channel_id=1, source_target_pairs={{4,0},{8,4},{12,8},{16,12},{20,16},{24,20},{28,24},{5,1},{9,5},{13... | collective-permute-start | bytes 147464 | tf_op jit(solution)/shard_map/ppermute | solution.py:19
  164.8 9.9 %copy-start.43 = (bf16[32,6,1,128]{3,0,2,1:T(8,128)(2,1)}, bf16[32,6,1,128]{3,0,2,1:T(8,128)(2,1)S(1)}, u32[]{:S(2)}) copy-start(bf16[32,6,1,128]{3,0,2,1:T(8,128)(2,1)S(1)} %collective-permute-done.14) | copy-start | bytes 147460
  188.3 21.9 %copy-start.55 = (bf16[32,6,1,128]{3,0,2,1:T(8,128)(2,1)}, bf16[32,6,1,128]{3,0,2,1:T(8,128)(2,1)S(1)}, u32[]{:S(2)}) copy-start(bf16[32,6,1,128]{3,0,2,1:T(8,128)(2,1)S(1)} %collective-permute-done.6) | copy-start | bytes 147460
  188.3 23.9 %copy-start.57 = (bf16[32,6,1,128]{3,0,2,1:T(8,128)(2,1)}, bf16[32,6,1,128]{3,0,2,1:T(8,128)(2,1)S(1)}, u32[]{:S(2)}) copy-start(bf16[32,6,1,128]{3,0,2,1:T(8,128)(2,1)S(1)} %collective-permute-done.7) | copy-start | bytes 147460
  626.9 3.6 copy-start.36
  626.9 3.6 copy-start.37
  626.9 3.6 copy-start.38
  626.9 3.6 copy-start.39
  626.9 3.6 copy-start.40
  627.0 3.6 copy-start.41
  627.0 3.6 copy-start.42
  (44 other events, 114.9 us)
where the time goes:
time: 647 us; the launch traced here: 646 us
  blocking collectives  499 us (77%)
  matrix products  80.8 us (12%)
  starting transfers between devices  46.4 us (7%)
  waiting for transfers between devices  7.08 us (1%)
    psum x1, blocking collectives, body(): lax.psum((local_one, local_bias, local_two), ('gx', 'gy'))  413 us
    dot_general x108, matrix products, conv_valid(): jnp.einsum('oi,ixyz->oxyz', weight[:, :, off_x, off_y, off_z], window, pr...  65.3 us
    all_gather x4, blocking collectives, full_padded(): gathered = lax.all_gather(values, 'af', axis=0, tiled=True)  59.7 us
    ppermute x8, starting transfers between devices, with_halo(): lax.ppermute(tail, axis, [(i, (i + 1) % count) for i in range(ends)])  35.7 us
    dot_general x54, matrix products, kernel_grad(): jnp.einsum('oxyz,ixyz->oi', cot_field, window, preferred_element_type=jnp...  15.6 us
    all_gather x1, blocking collectives, body(): lax.all_gather(weight_one, 'af', axis=0, tiled=True)  13 us
    all_gather x1, blocking collectives, body(): lax.all_gather(weight_two, 'af', axis=0, tiled=True)  13 us
  transfers between devices with their start and end apart: 16, of which 1 were waited for; matrix products, arithmetic and copies ran while one was open for 6% of the time, Pallas kernels for 0%

commit v1 on v0

v1 whole, which is shorter than its diff:
```python
import functools
import math

import jax
import jax.numpy as jnp
from jax import lax
from jax.experimental import pallas as pl
from jax.experimental.pallas import tpu as pltpu
from jax.sharding import PartitionSpec as P

MESH = pl.DeviceIdType.MESH
F32 = jnp.float32
BF16 = jnp.bfloat16

VOL, COT, HID, PRE = 0, 1, 2, 3
SIDES = [(dx, dy) for dx in (-1, 0, 1) for dy in (-1, 0, 1) if (dx, dy) != (0, 0)]
SEND = {-1: (1, 1), 0: (1, 4), 1: (4, 1)}
LAND = {-1: (5, 1), 0: (1, 4), 1: (0, 1)}


def iota(shape, dim):
    return lax.broadcasted_iota(jnp.int32, shape, dim)


def kernel(
    dims,
    vol, w_one, bias, w_two, cot,
    out, in_grad, g_one, g_bias, g_two,
    stage, got, w_stage, w_got, field, pre_act, lhs,
    out_stage, out_got, grad, core_got, core_sum, z_got, y_got, x_got, h_stage, h_got, final,
    in_send, in_recv, w_send, w_recv, halo_send, halo_recv, out_send, out_recv,
    core_send, core_recv, z_send, z_recv, y_send, y_recv, x_send, x_recv, h_send, h_recv,
):
    n_gx, n_gy = dims
    n_y, n_x = n_gx // 2, n_gy // 2
    gx, gy, af = lax.axis_index("gx"), lax.axis_index("gy"), lax.axis_index("af")
    row, core = gx // 2, gx % 2
    col, high = gy % n_x, gy // n_x

    def turned(at):
        even = (at % 2) == 0
        upper = at >= n_x
        return jnp.logical_xor(even, upper)

    def sub_of(at_af, at_gy):
        return jnp.where(turned(at_gy), 3 - at_af, at_af)

    sub = sub_of(af, gy)

    def y_neighbour(step):
        if step == 0:
            return gy, af
        inside = (sub < 3) if step > 0 else (sub > 0)
        gy_new = jnp.where(inside, gy, gy + step)
        sub_new = jnp.where(inside, sub + step, 0 if step > 0 else 3)
        return gy_new, sub_of(sub_new, gy_new)

    def has(dx, dy):
        checks = []
        if dx < 0:
            checks.append(gx > 0)
        if dx > 0:
            checks.append(gx < n_gx - 1)
        if dy < 0:
            checks.append(jnp.logical_or(gy > 0, sub > 0))
        if dy > 0:
            checks.append(jnp.logical_or(gy < n_gy - 1, sub < 3))
        if len(checks) == 1:
            return checks[0]
        return jnp.logical_and(checks[0], checks[1])

    neighbour = {}
    for dx, dy in SIDES:
        gy_new, af_new = y_neighbour(dy)
        neighbour[dx, dy] = {"gx": gx + dx, "gy": gy_new, "af": af_new}
    af_peer = [(af + k) % 4 for k in range(4)]

    zero_row = jnp.zeros((4, 6, 32, 128), BF16)
    for x in (0, 5):
        field[:, x] = zero_row
    for x in range(1, 5):
        for y in (0, 5):
            field[:, x, y] = jnp.zeros((4, 32, 128), BF16)
    grad[...] = jnp.zeros(grad.shape, F32)

    barrier = pltpu.get_barrier_semaphore()
    partners = [{"af": af_peer[k]} for k in range(1, 4)]
    partners += [{"gx": 2 * row + 1 - core}]
    partners += [{"gx": 2 * ((row + k) % n_y) + core} for k in range(1, n_y)]
    partners += [{"gy": high * n_x + (col + k) % n_x} for k in range(1, n_x)]
    partners += [{"gy": (1 - high) * n_x + col}]
    for partner in partners:
        pl.semaphore_signal(barrier, inc=1, device_id=partner, device_id_type=MESH)
    expected = jnp.int32(len(partners))
    for side in SIDES:

        @pl.when(has(*side))
        def _(side=side):
            pl.semaphore_signal(barrier, inc=1, device_id=neighbour[side], device_id_type=MESH)

        expected = expected + has(*side).astype(jnp.int32)

    r, q = iota((128, 128), 0), iota((128, 128), 1)
    to_wire = jnp.where(q == (r % 8) * 16 + r // 8, 1.0, 0.0).astype(BF16)
    from_wire = jnp.where(q == (r % 16) * 8 + r // 16, 1.0, 0.0).astype(BF16)

    def stage_input(which, source):
        block = jnp.concatenate([source[:, x].reshape(128, 128) for x in range(4)], axis=1)
        moved = jnp.dot(to_wire, block, preferred_element_type=F32).astype(BF16)
        for x in range(4):
            for j in range(4):
                part = moved[32 * j : 32 * j + 32, 128 * x : 128 * x + 128]
                stage[which, j, x] = part.reshape(2, 16, 128)
        got[which, pl.ds(af, 1)] = stage[which, pl.ds(sub, 1)]

    def in_copy(which, k):
        return pltpu.make_async_remote_copy(
            src_ref=stage.at[which, sub_of(af_peer[k], gy)],
            dst_ref=got.at[which, af],
            send_sem=in_send.at[which, k],
            recv_sem=in_recv.at[which, k],
            device_id={"af": af_peer[k]},
            device_id_type=MESH,
        )

    def w_copy(k):
        return pltpu.make_async_remote_copy(
            src_ref=w_stage,
            dst_ref=w_got.at[af],
            send_sem=w_send.at[k],
            recv_sem=w_recv.at[k],
            device_id={"af": af_peer[k]},
            device_id_type=MESH,
        )

    stage_input(VOL, vol)
    pl.semaphore_wait(barrier, expected)
    for k in (2, 1, 3):
        in_copy(VOL, k).start()

    diag = iota((8, 8), 0) == iota((8, 8), 1)
    bias_col = jnp.sum(jnp.where(diag, bias[...], 0.0), axis=1, keepdims=True)
    part_a = bias_col.astype(BF16).astype(F32)
    part_b = (bias_col - part_a).astype(BF16).astype(F32)
    part_c = (bias_col - part_a) - part_b
    lane32 = iota((8, 32), 1)
    spare = jnp.where(lane32 == 0, part_a, jnp.where(lane32 == 1, part_b, jnp.where(lane32 == 2, part_c, 0.0)))
    for which, weight in enumerate((w_one, w_two)):
        groups = []
        for a in range(7):
            taps = []
            for b in range(4):
                t = 4 * a + b
                taps.append(weight[t // 9, (t // 3) % 3, t % 3].astype(F32) if t < 27 else spare)
            groups.append(jnp.concatenate(taps, axis=1))
        groups.append(jnp.zeros((8, 128), F32))
        packed = jnp.concatenate(groups, axis=0).astype(BF16)
        w_stage[which] = packed
        w_got[af, which] = packed
    for k in (2, 1, 3):
        w_copy(k).start()
    stage_input(COT, cot)
    for k in (2, 1, 3):
        in_copy(COT, k).start()

    def halo_copy(which, side):
        number = SIDES.index(side)
        (sx, nx), (sy, ny) = SEND[side[0]], SEND[side[1]]
        (lx, _), (ly, _) = LAND[side[0]], LAND[side[1]]
        return pltpu.make_async_remote_copy(
            src_ref=field.at[which, sx : sx + nx, sy : sy + ny],
            dst_ref=field.at[which, lx : lx + nx, ly : ly + ny],
            send_sem=halo_send.at[which, number],
            recv_sem=halo_recv.at[which, number],
            device_id=neighbour[side],
            device_id_type=MESH,
        )

    def halo_start(which):
        for side in SIDES:

            @pl.when(has(*side))
            def _(side=side):
                halo_copy(which, side).start()

    def halo_wait(which):
        for side in SIDES:

            @pl.when(has(-side[0], -side[1]))
            def _(side=side):
                halo_copy(which, side).wait_recv()

    def assemble(which):
        for x in range(4):
            for pair in range(2):
                parts = [got[which, s, x, pair].astype(F32) for s in range(4)]
                for odd in range(2):
                    rows = [part[8 * odd : 8 * odd + 8] for part in parts]
                    field[which, 1 + x, 1 + 2 * pair + odd] = jnp.concatenate(rows, axis=0).astype(BF16)

    for k in range(1, 4):
        in_copy(VOL, k).wait_recv()
    assemble(VOL)
    halo_start(VOL)

    for k in range(1, 4):
        w_copy(k).wait_recv()

    def taps_of(which):
        parts = [w_got[s, which].astype(F32) for s in range(4)]
        groups = [
            jnp.concatenate([part[8 * a : 8 * a + 8] for part in parts], axis=0) for a in range(7)
        ]

        def tap(dx, dy, dz):
            t = (dx * 3 + dy) * 3 + dz
            return groups[t // 4][:, 32 * (t % 4) : 32 * (t % 4) + 32]

        return groups, tap

    def make_forward(which):
        groups, tap = taps_of(which)
        for dz in range(3):
            line = jnp.concatenate([tap(k // 3, k % 3, dz) for k in range(9)], axis=1)
            lhs[2 * which, 32 * dz : 32 * dz + 32] = line.astype(BF16)
        return groups

    def make_turned(which):
        _, tap = taps_of(which)
        zeros = jnp.zeros((32, 32), F32)
        for dx in range(3):
            lines = [
                jnp.concatenate([tap(2 - dx, 2 - dy, 2 - dz) for dz in range(3)] + [zeros], axis=1)
                for dy in range(3)
            ]
            lines.append(jnp.zeros((32, 128), F32))
            block = jnp.concatenate(lines, axis=0)
            lhs[2 * which + 1, :, 96 * dx : 96 * dx + 96] = block.T[:96, :96].astype(BF16)

    groups = make_forward(0)
    bias_all = groups[6][:, 96:97] + groups[6][:, 97:98] + groups[6][:, 98:99]
    make_turned(1)

    lane = iota((32, 128), 1)
    not_first = lane > 0
    not_last = lane < 127

    def shift_up(rows):
        return jnp.where(not_first, pltpu.roll(rows, 1, 1), 0.0)

    def shift_down(rows):
        return jnp.where(not_last, pltpu.roll(rows, 127, 1), 0.0)

    def window(which, x, dx):
        return jnp.concatenate(
            [field[which, x + dx, y : y + 3].reshape(96, 128) for y in range(4)], axis=1
        )

    def conv(which, number, x):
        block = jnp.concatenate([window(which, x, dx) for dx in range(3)], axis=0)
        sums = jnp.dot(lhs[number], block, preferred_element_type=F32)
        lines = []
        for y in range(4):
            part = sums[:, 128 * y : 128 * y + 128]
            lines.append(part[32:64] + shift_up(part[0:32]) + shift_down(part[64:96]))
        return lines

    halo_wait(VOL)
    for x in range(4):
        for y, line in enumerate(conv(VOL, 0, x)):
            act = line + bias_all
            pre_act[x, y] = act
            field[HID, 1 + x, 1 + y] = (act / (1.0 + jnp.exp(-act))).astype(BF16)
    halo_start(HID)

    for k in range(1, 4):
        in_copy(COT, k).wait_recv()
    assemble(COT)
    halo_start(COT)
    make_forward(1)
    make_turned(0)
    halo_wait(COT)
    bias_sum = jnp.zeros((32, 128), F32)
    for x in range(4):
        for y, line in enumerate(conv(COT, 3, x)):
            act = pre_act[x, y]
            sig = 1.0 / (1.0 + jnp.exp(-act))
            value = (line * sig * (1.0 + act * (1.0 - sig))).astype(BF16)
            bias_sum = bias_sum + value.astype(F32)
            field[PRE, 1 + x, 1 + y] = value
    halo_start(PRE)

    def shifted(which, x, flip):
        columns = []
        for y in range(4):
            rows = field[which, 1 + x, 1 + y].astype(F32)
            up, down = shift_up(rows), shift_down(rows)
            trio = [down, rows, up] if flip else [up, rows, down]
            columns.append(jnp.concatenate(trio, axis=0).astype(BF16))
        return jnp.concatenate(columns, axis=1)

    along = (((1,), (1,)), ((), ()))

    acc_one = [jnp.zeros((96, 96), F32) for _ in range(3)]
    acc_two = [jnp.zeros((96, 96), F32) for _ in range(3)]
    for x in range(4):
        own_pre = shifted(PRE, x, True)
        own_hid = shifted(HID, x, False)
        for dx in range(3):
            acc_one[dx] = acc_one[dx] + lax.dot_general(
                own_pre, window(VOL, x, dx), along, preferred_element_type=F32
            )
            acc_two[dx] = acc_two[dx] + lax.dot_general(
                window(COT, x, dx), own_hid, along, preferred_element_type=F32
            )
    bias_own = jnp.sum(bias_sum, axis=1, keepdims=True)
    for dx in range(3):
        for k in range(3):
            for s in range(4):
                rows = slice(32 * k + 8 * s, 32 * k + 8 * s + 8)
                grad[0, s, 3 * dx + k, :, 0:96] = acc_one[dx][rows]
                grad[1, s, 3 * dx + k, :, 0:96] = acc_two[dx][rows]
    for s in range(4):
        grad[0, s, 0, :, 96:97] = bias_own[8 * s : 8 * s + 8]

    core_copy = pltpu.make_async_remote_copy(
        src_ref=grad.at[1 - core],
        dst_ref=core_got,
        send_sem=core_send.at[0],
        recv_sem=core_recv.at[0],
        device_id={"gx": 2 * row + 1 - core},
        device_id_type=MESH,
    )
    core_copy.start()

    def out_copy(which, k):
        return pltpu.make_async_remote_copy(
            src_ref=out_stage.at[which, af_peer[k]],
            dst_ref=out_got.at[which, sub],
            send_sem=out_send.at[which, k],
            recv_sem=out_recv.at[which, k],
            device_id={"af": af_peer[k]},
            device_id_type=MESH,
        )

    def produce(which, source, number):
        for x in range(4):
            lines = conv(source, number, x)
            for pair in range(2):
                for s in range(4):
                    rows = [lines[2 * pair + odd][8 * s : 8 * s + 8] for odd in range(2)]
                    out_stage[which, s, x, pair] = jnp.concatenate(rows, axis=0).astype(BF16)
        out_got[which, pl.ds(sub, 1)] = out_stage[which, pl.ds(af, 1)]
        for k in (2, 1, 3):
            out_copy(which, k).start()

    halo_wait(HID)
    produce(0, HID, 2)

    core_copy.wait_recv()
    core_sum[...] = grad[core] + core_got[...]
    z_got[af] = core_sum[af]

    def z_copy(k):
        return pltpu.make_async_remote_copy(
            src_ref=core_sum.at[af_peer[k]],
            dst_ref=z_got.at[af],
            send_sem=z_send.at[k],
            recv_sem=z_recv.at[k],
            device_id={"af": af_peer[k]},
            device_id_type=MESH,
        )

    for k in range(1, 4):
        z_copy(k).start()

    halo_wait(PRE)
    produce(1, PRE, 1)

    for k in range(1, 4):
        z_copy(k).wait_recv()
    y_got[row] = z_got[0] + z_got[1] + z_got[2] + z_got[3]

    def y_copy(k):
        return pltpu.make_async_remote_copy(
            src_ref=y_got.at[row],
            dst_ref=y_got.at[row],
            send_sem=y_send.at[k],
            recv_sem=y_recv.at[k],
            device_id={"gx": 2 * ((row + k) % n_y) + core},
            device_id_type=MESH,
        )

    for k in range(1, n_y):
        y_copy(k).start()
    for k in range(1, n_y):
        y_copy(k).wait_recv()
    x_got[col] = sum([y_got[i] for i in range(1, n_y)], y_got[0])

    def x_copy(k):
        return pltpu.make_async_remote_copy(
            src_ref=x_got.at[col],
            dst_ref=x_got.at[col],
            send_sem=x_send.at[k],
            recv_sem=x_recv.at[k],
            device_id={"gy": high * n_x + (col + k) % n_x},
            device_id_type=MESH,
        )

    for k in range(1, n_x):
        x_copy(k).start()
    for k in range(1, n_x):
        x_copy(k).wait_recv()
    h_stage[...] = sum([x_got[i] for i in range(1, n_x)], x_got[0])
    h_copy = pltpu.make_async_remote_copy(
        src_ref=h_stage,
        dst_ref=h_got,
        send_sem=h_send.at[0],
        recv_sem=h_recv.at[0],
        device_id={"gy": (1 - high) * n_x + col},
        device_id_type=MESH,
    )
    h_copy.start()

    def finish(which, target):
        for k in range(1, 4):
            out_copy(which, k).wait_recv()
        block = jnp.concatenate(
            [
                jnp.concatenate([out_got[which, j, x].reshape(32, 128) for j in range(4)], axis=0)
                for x in range(4)
            ],
            axis=1,
        )
        moved = jnp.dot(from_wire, block, preferred_element_type=F32).astype(BF16)
        for x in range(4):
            target[:, x] = moved[:, 128 * x : 128 * x + 128].reshape(8, 16, 128)

    finish(0, out)
    h_copy.wait_recv()
    scale = 1.0 / math.sqrt(4 * n_gx * 16 * n_gy * 128)
    final[core] = (h_stage[...] + h_got[...]) * scale
    last_copy = pltpu.make_async_remote_copy(
        src_ref=final.at[core],
        dst_ref=final.at[core],
        send_sem=core_send.at[1],
        recv_sem=core_recv.at[1],
        device_id={"gx": 2 * row + 1 - core},
        device_id_type=MESH,
    )
    last_copy.start()
    finish(1, in_grad)
    last_copy.wait_recv()
    for dx in range(3):
        for k in range(3):
            tile_one = final[0, 3 * dx + k]
            tile_two = final[1, 3 * dx + k]
            for m in range(3):
                g_one[dx, m, k] = tile_one[:, 32 * m : 32 * m + 32]
                g_two[2 - dx, 2 - k, m] = tile_two[:, 32 * m : 32 * m + 32]
    g_bias[...] = final[0, 0][:, 96:97]

    for k in range(1, 4):
        in_copy(VOL, k).wait_send()
        in_copy(COT, k).wait_send()
        w_copy(k).wait_send()
        out_copy(0, k).wait_send()
        out_copy(1, k).wait_send()
        z_copy(k).wait_send()
    for which in (VOL, COT, HID, PRE):
        for side in SIDES:

            @pl.when(has(*side))
            def _(which=which, side=side):
                halo_copy(which, side).wait_send()

    core_copy.wait_send()
    for k in range(1, n_y):
        y_copy(k).wait_send()
    for k in range(1, n_x):
        x_copy(k).wait_send()
    h_copy.wait_send()
    last_copy.wait_send()


def body(dims, volume, weight_one, bias_one, weight_two, cotangent):
    n_y, n_x = dims[0] // 2, dims[1] // 2
    as_taps = (2, 3, 4, 0, 1)
    dma = pltpu.SemaphoreType.DMA
    out, in_grad, g_one, g_bias, g_two = pl.pallas_call(
        functools.partial(kernel, dims),
        out_shape=(
            jax.ShapeDtypeStruct((8, 4, 16, 128), BF16),
            jax.ShapeDtypeStruct((8, 4, 16, 128), BF16),
            jax.ShapeDtypeStruct((3, 3, 3, 8, 32), F32),
            jax.ShapeDtypeStruct((8, 1), F32),
            jax.ShapeDtypeStruct((3, 3, 3, 8, 32), F32),
        ),
        in_specs=[pl.BlockSpec(memory_space=pltpu.VMEM)] * 5,
        out_specs=[pl.BlockSpec(memory_space=pltpu.VMEM)] * 5,
        scratch_shapes=[
            pltpu.VMEM((2, 4, 4, 2, 16, 128), BF16),
            pltpu.VMEM((2, 4, 4, 2, 16, 128), BF16),
            pltpu.VMEM((2, 64, 128), BF16),
            pltpu.VMEM((4, 2, 64, 128), BF16),
            pltpu.VMEM((4, 6, 6, 32, 128), BF16),
            pltpu.VMEM((4, 4, 32, 128), F32),
            pltpu.VMEM((4, 96, 288), BF16),
            pltpu.VMEM((2, 4, 4, 2, 16, 128), BF16),
            pltpu.VMEM((2, 4, 4, 2, 16, 128), BF16),
            pltpu.VMEM((2, 4, 9, 8, 128), F32),
            pltpu.VMEM((4, 9, 8, 128), F32),
            pltpu.VMEM((4, 9, 8, 128), F32),
            pltpu.VMEM((4, 9, 8, 128), F32),
            pltpu.VMEM((n_y, 9, 8, 128), F32),
            pltpu.VMEM((n_x, 9, 8, 128), F32),
            pltpu.VMEM((9, 8, 128), F32),
            pltpu.VMEM((9, 8, 128), F32),
            pltpu.VMEM((2, 9, 8, 128), F32),
            dma((2, 4)), dma((2, 4)), dma((4,)), dma((4,)), dma((4, 8)), dma((4, 8)), dma((2, 4)), dma((2, 4)),
            dma((2,)), dma((2,)), dma((4,)), dma((4,)), dma((4,)), dma((4,)), dma((4,)), dma((4,)), dma((1,)), dma((1,)),
        ],
        compiler_params=pltpu.CompilerParams(
            collective_id=0, has_side_effects=True, vmem_limit_bytes=32 * 1024 * 1024
        ),
    )(
        volume,
        jnp.transpose(weight_one, as_taps),
        bias_one.reshape(1, 8),
        jnp.transpose(weight_two, as_taps),
        cotangent,
    )
    as_given = (3, 4, 0, 1, 2)
    return (
        out,
        in_grad,
        jnp.transpose(g_one, as_given),
        g_bias.reshape(8),
        jnp.transpose(g_two, as_given),
    )


def solution(mesh):
    dims = (mesh.shape["gx"], mesh.shape["gy"])
    return jax.shard_map(
        functools.partial(body, dims),
        mesh=mesh,
        in_specs=(
            P("af", "gx", "gy", None),
            P("af", None, None, None, None),
            P("af"),
            P("af", None, None, None, None),
            P("af", "gx", "gy", None),
        ),
        out_specs=(
            P("af", "gx", "gy", None),
            P("af", "gx", "gy", None),
            P("af", None, None, None, None),
            P("af"),
            P("af", None, None, None, None),
        ),
        check_vma=False,
    )
```

time: 647 us -> 61.2 us (0.09)
  the two profiles are of different devices: /device:TPU:0 before, /device:TPU:1 now
where the time goes in v1:
time: 61.2 us; the launch traced here: 61 us
  Pallas kernels  53 us (87%)
  local copies, waits for them, and re-layouts  6.68 us (11%)
  between operations  0.66 us (1%)
  other arithmetic  0.63 us (1%)
    pallas_call x1, Pallas kernels, body(): pl.pallas_call(functools.partial(kernel, dims), out_shape=(jax.ShapeDtype...  53 us
    unnamed x14, local copies, waits for them, and re-layouts  6.68 us

profile of v1, /device:TPU:1, one launch (start us, length us, event | category | flops | bytes accessed | tf_op | source)
XLA Modules:
  0.0 61.0 jit_solution(12851599947450968906)
XLA Ops:
  0.6 0.0 copy-start.4
  0.6 0.6 %copy-done.4 = f32[8]{0:T(128)S(1)} copy-done((f32[8]{0:T(128)S(1)}, f32[8]{0:T(128)}, u32[]{:S(2)}) %copy-start.4) | copy-done | bytes 56
  1.3 0.0 copy-start
  1.3 0.9 %copy-done = bf16[8,4,16,128]{3,2,1,0:T(8,128)(2,1)S(1)} copy-done((bf16[8,4,16,128]{3,2,1,0:T(8,128)(2,1)S(1)}, bf16[8,4,16,128]{3,2,1,0:T(8,128)(2,1)}, u32[]{:S(2)}) %copy-start) | copy-done | bytes 131096
  2.2 0.0 copy-start.1
  2.2 0.9 %copy-done.1 = bf16[8,4,16,128]{3,2,1,0:T(8,128)(2,1)S(1)} copy-done((bf16[8,4,16,128]{3,2,1,0:T(8,128)(2,1)S(1)}, bf16[8,4,16,128]{3,2,1,0:T(8,128)(2,1)}, u32[]{:S(2)}) %copy-start.1) | copy-done | bytes 131096
  3.1 0.0 copy-start.2
  3.1 0.8 %copy-done.2 = bf16[8,32,3,3,3]{1,0,4,3,2:T(8,128)(2,1)S(1)} copy-done((bf16[8,32,3,3,3]{1,0,4,3,2:T(8,128)(2,1)S(1)}, bf16[8,32,3,3,3]{1,0,4,3,2:T(8,128)(2,1)}, u32[]{:S(2)}) %copy-start.2) | copy-done | bytes 13848
  3.9 0.0 copy-start.3
  3.9 0.8 %copy-done.3 = bf16[8,32,3,3,3]{1,0,4,3,2:T(8,128)(2,1)S(1)} copy-done((bf16[8,32,3,3,3]{1,0,4,3,2:T(8,128)(2,1)S(1)}, bf16[8,32,3,3,3]{1,0,4,3,2:T(8,128)(2,1)}, u32[]{:S(2)}) %copy-start.3) | copy-done | bytes 13848
  4.7 53.0 %shard_map.92 = (bf16[8,4,16,128]{3,2,1,0:T(8,128)(2,1)S(1)}, bf16[8,4,16,128]{3,2,1,0:T(8,128)(2,1)S(1)}, f32[3,3,3,8,32]{4,3,2,1,0:T(8,128)S(1)}, f32[8,1]{1,0:T(8,128)S(1)}, f32[3,3,3,8,32]{4,3,2,1,0:T(8,128)S(1)}) custom-call(bf16[8,4,16,128]{3,2,1,0:T(8,128)(2,1)S(1)} %copy-done, bf16[3,3,3,8,32]{4,3,2,1,0:T(8,128)(2,1)S(1)} %bitcast.7, ...), custom_call_target="tpu_custom_call" | custom-call | tf_op jit(solution)/shard_map/pallas_call | solution.py:490
  57.8 0.6 %reduce = f32[8]{0:T(128)} reduce(f32[8,1]{1,0:T(8,128)S(1)} %get-tuple-element.13, f32[]{:T(128)} %constant.2), dimensions={1}, to_apply=%get-tuple-element.13.reduce_sub_computation | reduce | bytes 68 | tf_op jit(solution)/shard_map/pallas_call | solution.py:490
  58.4 0.7 %copy.14 = bf16[8,4,16,128]{3,2,1,0:T(8,128)(2,1)} copy(bf16[8,4,16,128]{3,2,1,0:T(8,128)(2,1)S(1)} %get-tuple-element.20) | data formatting | bytes 262144
  59.0 0.7 %copy.15 = bf16[8,4,16,128]{3,2,1,0:T(8,128)(2,1)} copy(bf16[8,4,16,128]{3,2,1,0:T(8,128)(2,1)S(1)} %get-tuple-element.21) | data formatting | bytes 262144
  59.7 0.6 %copy.16 = f32[8,32,3,3,3]{1,0,4,3,2:T(8,128)} copy(f32[8,32,3,3,3]{1,0,4,3,2:T(8,128)S(1)} %bitcast.6) | data formatting | bytes 55296
  60.3 0.6 %copy.17 = f32[8,32,3,3,3]{1,0,4,3,2:T(8,128)} copy(f32[8,32,3,3,3]{1,0,4,3,2:T(8,128)S(1)} %bitcast.5) | data formatting | bytes 55296
Async XLA Ops:
  0.6 0.7 %copy-start.4 = (f32[8]{0:T(128)S(1)}, f32[8]{0:T(128)}, u32[]{:S(2)}) copy-start(f32[8]{0:T(128)} %param.7) | copy-start | bytes 100
  1.3 0.9 %copy-start = (bf16[8,4,16,128]{3,2,1,0:T(8,128)(2,1)S(1)}, bf16[8,4,16,128]{3,2,1,0:T(8,128)(2,1)}, u32[]{:S(2)}) copy-start(bf16[8,4,16,128]{3,2,1,0:T(8,128)(2,1)} %vol.1) | copy-start | bytes 393220
  2.2 0.9 %copy-start.1 = (bf16[8,4,16,128]{3,2,1,0:T(8,128)(2,1)S(1)}, bf16[8,4,16,128]{3,2,1,0:T(8,128)(2,1)}, u32[]{:S(2)}) copy-start(bf16[8,4,16,128]{3,2,1,0:T(8,128)(2,1)} %cot.1) | copy-start | bytes 393220
  3.1 0.8 %copy-start.2 = (bf16[8,32,3,3,3]{1,0,4,3,2:T(8,128)(2,1)S(1)}, bf16[8,32,3,3,3]{1,0,4,3,2:T(8,128)(2,1)}, u32[]{:S(2)}) copy-start(bf16[8,32,3,3,3]{1,0,4,3,2:T(8,128)(2,1)} %param.6) | copy-start | bytes 41476
  3.9 0.8 %copy-start.3 = (bf16[8,32,3,3,3]{1,0,4,3,2:T(8,128)(2,1)S(1)}, bf16[8,32,3,3,3]{1,0,4,3,2:T(8,128)(2,1)}, u32[]{:S(2)}) copy-start(bf16[8,32,3,3,3]{1,0,4,3,2:T(8,128)(2,1)} %param.8) | copy-start | bytes 41476

commit v2 on v1

--- a/solution.py
+++ b/solution.py
@@ -24,13 +24,29 @@
 
 def kernel(
     dims,
+    vol_in, w_one_in, bias_in, w_two_in, cot_in,
+    out_to, in_grad_to, g_one_to, g_bias_to, g_two_to,
+    out, in_grad, g_one, g_bias, g_two,
     vol, w_one, bias, w_two, cot,
-    out, in_grad, g_one, g_bias, g_two,
     stage, got, w_stage, w_got, field, pre_act, lhs,
     out_stage, out_got, grad, core_got, core_sum, z_got, y_got, x_got, h_stage, h_got, final,
     in_send, in_recv, w_send, w_recv, halo_send, halo_recv, out_send, out_recv,
-    core_send, core_recv, z_send, z_recv, y_send, y_recv, x_send, x_recv, h_send, h_recv,
+    core_send, core_recv, z_send, z_recv, y_send, y_recv, x_send, x_recv, h_send, h_recv, load_sem, store_sem,
 ):
+    loads = [
+        pltpu.make_async_copy(source, target, load_sem.at[i])
+        for i, (source, target) in enumerate(
+            ((vol_in, vol), (w_one_in, w_one), (w_two_in, w_two), (bias_in, bias), (cot_in, cot))
+        )
+    ]
+    for load in loads:
+        load.start()
+    stores = [
+        pltpu.make_async_copy(source, target, store_sem.at[i])
+        for i, (source, target) in enumerate(
+            ((out, out_to), (in_grad, in_grad_to), (g_one, g_one_to), (g_bias, g_bias_to), (g_two, g_two_to))
+        )
+    ]
     n_gx, n_gy = dims
     n_y, n_x = n_gx // 2, n_gy // 2
     gx, gy, af = lax.axis_index("gx"), lax.axis_index("gy"), lax.axis_index("af")
@@ -133,11 +149,14 @@
             device_id_type=MESH,
         )
 
+    loads[0].wait()
     stage_input(VOL, vol)
     pl.semaphore_wait(barrier, expected)
     for k in (2, 1, 3):
         in_copy(VOL, k).start()
 
+    for load in loads[1:]:
+        load.wait()
     diag = iota((8, 8), 0) == iota((8, 8), 1)
     bias_col = jnp.sum(jnp.where(diag, bias[...], 0.0), axis=1, keepdims=True)
     part_a = bias_col.astype(BF16).astype(F32)
@@ -437,6 +456,7 @@
             target[:, x] = moved[:, 128 * x : 128 * x + 128].reshape(8, 16, 128)
 
     finish(0, out)
+    stores[0].start()
     h_copy.wait_recv()
     scale = 1.0 / math.sqrt(4 * n_gx * 16 * n_gy * 128)
     final[core] = (h_stage[...] + h_got[...]) * scale
@@ -450,6 +470,7 @@
     )
     last_copy.start()
     finish(1, in_grad)
+    stores[1].start()
     last_copy.wait_recv()
     for dx in range(3):
         for k in range(3):
@@ -458,7 +479,9 @@
             for m in range(3):
                 g_one[dx, m, k] = tile_one[:, 32 * m : 32 * m + 32]
                 g_two[2 - dx, 2 - k, m] = tile_two[:, 32 * m : 32 * m + 32]
-    g_bias[...] = final[0, 0][:, 96:97]
+    g_bias[...] = jnp.sum(jnp.where(diag, final[0, 0][:, 96:97], 0.0), axis=0, keepdims=True)
+    for copy in stores[2:]:
+        copy.start()
 
     for k in range(1, 4):
         in_copy(VOL, k).wait_send()
@@ -481,6 +504,20 @@
         x_copy(k).wait_send()
     h_copy.wait_send()
     last_copy.wait_send()
+    for copy in stores:
+        copy.wait()
+
+
+def store(*refs):
+    sources, targets, sems = refs[:5], refs[5:10], refs[10]
+    copies = [
+        pltpu.make_async_copy(source, target, sems.at[i])
+        for i, (source, target) in enumerate(zip(sources, targets))
+    ]
+    for copy in copies:
+        copy.start()
+    for copy in copies:
+        copy.wait()
 
 
 def body(dims, volume, weight_one, bias_one, weight_two, cotangent):
@@ -493,12 +530,22 @@
             jax.ShapeDtypeStruct((8, 4, 16, 128), BF16),
             jax.ShapeDtypeStruct((8, 4, 16, 128), BF16),
             jax.ShapeDtypeStruct((3, 3, 3, 8, 32), F32),
-            jax.ShapeDtypeStruct((8, 1), F32),
+            jax.ShapeDtypeStruct((1, 8), F32),
             jax.ShapeDtypeStruct((3, 3, 3, 8, 32), F32),
         ),
-        in_specs=[pl.BlockSpec(memory_space=pltpu.VMEM)] * 5,
-        out_specs=[pl.BlockSpec(memory_space=pltpu.VMEM)] * 5,
+        in_specs=[pl.BlockSpec(memory_space=pltpu.HBM)] * 5,
+        out_specs=[pl.BlockSpec(memory_space=pltpu.HBM)] * 5,
         scratch_shapes=[
+            pltpu.VMEM((8, 4, 16, 128), BF16),
+            pltpu.VMEM((8, 4, 16, 128), BF16),
+            pltpu.VMEM((3, 3, 3, 8, 32), F32),
+            pltpu.VMEM((1, 8), F32),
+            pltpu.VMEM((3, 3, 3, 8, 32), F32),
+            pltpu.VMEM((8, 4, 16, 128), BF16),
+            pltpu.VMEM((3, 3, 3, 8, 32), BF16),
+            pltpu.VMEM((1, 8), F32),
+            pltpu.VMEM((3, 3, 3, 8, 32), BF16),
+            pltpu.VMEM((8, 4, 16, 128), BF16),
             pltpu.VMEM((2, 4, 4, 2, 16, 128), BF16),
             pltpu.VMEM((2, 4, 4, 2, 16, 128), BF16),
             pltpu.VMEM((2, 64, 128), BF16),
@@ -519,9 +566,10 @@
             pltpu.VMEM((2, 9, 8, 128), F32),
             dma((2, 4)), dma((2, 4)), dma((4,)), dma((4,)), dma((4, 8)), dma((4, 8)), dma((2, 4)), dma((2, 4)),
             dma((2,)), dma((2,)), dma((4,)), dma((4,)), dma((4,)), dma((4,)), dma((4,)), dma((4,)), dma((1,)), dma((1,)),
+            dma((5,)), dma((5,)),
         ],
         compiler_params=pltpu.CompilerParams(
-            collective_id=0, has_side_effects=True, vmem_limit_bytes=32 * 1024 * 1024
+            collective_id=0, has_side_effects=True, vmem_limit_bytes=60 * 1024 * 1024
         ),
     )(
         volume,
@@ -530,6 +578,15 @@
         jnp.transpose(weight_two, as_taps),
         cotangent,
     )
+    results = (out, in_grad, g_one, g_bias, g_two)
+    out, in_grad, g_one, g_bias, g_two = pl.pallas_call(
+        store,
+        out_shape=tuple(jax.ShapeDtypeStruct(part.shape, part.dtype) for part in results),
+        in_specs=[pl.BlockSpec(memory_space=pltpu.HBM)] * 5,
+        out_specs=[pl.BlockSpec(memory_space=pltpu.HBM)] * 5,
+        scratch_shapes=[dma((5,))],
+        compiler_params=pltpu.CompilerParams(vmem_limit_bytes=60 * 1024 * 1024),
+    )(*results)
     as_given = (3, 4, 0, 1, 2)
     return (
         out,

time: 61.2 us -> 70.2 us (1.15)
  Pallas kernels: 53 us -> 69.5 us
  local copies, waits for them, and re-layouts: 6.68 us -> 0 us
    pallas_call x0 -> x1, Pallas kernels: none -> 15.8 us  [body(): pl.pallas_call(store, out_shape=tuple((jax.ShapeDtypeStruct(part.shape, p...]
    unnamed x14 -> x0, local copies, waits for them, and re-layouts: 6.68 us -> none
where the time goes in v2:
time: 70.2 us
  Pallas kernels  69.5 us (99%)
    pallas_call x1, Pallas kernels, body(): pl.pallas_call(functools.partial(kernel, dims), out_shape=(jax.ShapeDtype...  53.7 us
    pallas_call x1, Pallas kernels, body(): pl.pallas_call(store, out_shape=tuple((jax.ShapeDtypeStruct(part.shape, p...  15.8 us

profile of v2, /device:TPU:1, one launch (start us, length us, event | category | flops | bytes accessed | tf_op | source)
XLA Modules:
  0.0 70.2 jit_solution(9187526077958267474)
XLA Ops:
  0.6 53.7 %shard_map.92 = (bf16[8,4,16,128]{3,2,1,0:T(8,128)(2,1)}, bf16[8,4,16,128]{3,2,1,0:T(8,128)(2,1)}, f32[3,3,3,8,32]{4,3,2,1,0:T(8,128)}, f32[1,8]{1,0:T(1,128)}, f32[3,3,3,8,32]{4,3,2,1,0:T(8,128)}) custom-call(bf16[8,4,16,128]{3,2,1,0:T(8,128)(2,1)} %vol_in.1, bf16[3,3,3,8,32]{4,3,2,1,0:T(8,128)(2,1)} %bitcast.6, f32[1,8]{1,0:T(1,128)} %bitcast.8, ...), custom_call_target="tpu_custom_call" | custom-call | tf_op jit(solution)/shard_map/pallas_call | solution.py:527
  54.3 15.8 %shard_map.93 = (bf16[8,4,16,128]{3,2,1,0:T(8,128)(2,1)}, bf16[8,4,16,128]{3,2,1,0:T(8,128)(2,1)}, f32[3,3,3,8,32]{4,3,2,1,0:T(8,128)}, f32[1,8]{1,0:T(1,128)}, f32[3,3,3,8,32]{4,3,2,1,0:T(8,128)}) custom-call(bf16[8,4,16,128]{3,2,1,0:T(8,128)(2,1)} %get-tuple-element.15.refs_0_, bf16[8,4,16,128]{3,2,1,0:T(8,128)(2,1)} %get-tuple-element.16.refs_1_, ...), custom_call_target="tpu_custom_call" | custom-call | tf_op jit(solution)/shard_map/pallas_call | solution.py:582

commit v3 on v2

--- a/solution.py
+++ b/solution.py
@@ -15,6 +15,7 @@
 VOL, COT, HID, PRE = 0, 1, 2, 3
 SIDES = [(dx, dy) for dx in (-1, 0, 1) for dy in (-1, 0, 1) if (dx, dy) != (0, 0)]
 SEND = {-1: (1, 1), 0: (1, 4), 1: (4, 1)}
+EDGE = {-1: (0, 1), 0: (1, 4), 1: (5, 1)}
 LAND = {-1: (5, 1), 0: (1, 4), 1: (0, 1)}
 
 
@@ -29,9 +30,9 @@
     out, in_grad, g_one, g_bias, g_two,
     vol, w_one, bias, w_two, cot,
     stage, got, w_stage, w_got, field, pre_act, lhs,
-    out_stage, out_got, grad, core_got, core_sum, z_got, y_got, x_got, h_stage, h_got, final,
-    in_send, in_recv, w_send, w_recv, halo_send, halo_recv, out_send, out_recv,
-    core_send, core_recv, z_send, z_recv, y_send, y_recv, x_send, x_recv, h_send, h_recv, load_sem, store_sem,
+    out_stage, out_got, grad, core_got, core_sum, plane_got, line_stage, line_got, final,
+    in_send, in_recv, w_send, w_recv, pass_send, pass_recv, halo_send, halo_recv, out_send, out_recv,
+    core_send, core_recv, plane_send, plane_recv, line_send, line_recv, last_send, last_recv, load_sem, store_sem,
 ):
     loads = [
         pltpu.make_async_copy(source, target, load_sem.at[i])
@@ -91,20 +92,23 @@
         neighbour[dx, dy] = {"gx": gx + dx, "gy": gy_new, "af": af_new}
     af_peer = [(af + k) % 4 for k in range(4)]
 
-    zero_row = jnp.zeros((4, 6, 32, 128), BF16)
-    for x in (0, 5):
-        field[:, x] = zero_row
-    for x in range(1, 5):
-        for y in (0, 5):
-            field[:, x, y] = jnp.zeros((4, 32, 128), BF16)
-    grad[...] = jnp.zeros(grad.shape, F32)
+    plane = n_y * n_x
+    place = row * n_x + col
+    kept = 16 // plane
+
+    def at_place(k):
+        other = (place + k) % plane
+        return other // n_x, high * n_x + other % n_x
 
     barrier = pltpu.get_barrier_semaphore()
-    partners = [{"af": af_peer[k]} for k in range(1, 4)]
-    partners += [{"gx": 2 * row + 1 - core}]
-    partners += [{"gx": 2 * ((row + k) % n_y) + core} for k in range(1, n_y)]
-    partners += [{"gy": high * n_x + (col + k) % n_x} for k in range(1, n_x)]
-    partners += [{"gy": (1 - high) * n_x + col}]
+    partners = []
+    for k in range(plane):
+        other_row, other_gy = at_place(k)
+        for other_core in (1 - core, core):
+            partners.append({"gx": 2 * other_row + other_core, "gy": other_gy, "af": af})
+    partners.pop(1)
+    for k in range(1, 8):
+        partners.append({"gx": gx, "gy": ((high + k // 4) % 2) * n_x + col, "af": af_peer[k % 4]})
     for partner in partners:
         pl.semaphore_signal(barrier, inc=1, device_id=partner, device_id_type=MESH)
     expected = jnp.int32(len(partners))
@@ -115,6 +119,11 @@
             pl.semaphore_signal(barrier, inc=1, device_id=neighbour[side], device_id_type=MESH)
 
         expected = expected + has(*side).astype(jnp.int32)
+
+        @pl.when(jnp.logical_not(has(*side)))
+        def _(side=side):
+            (fx, cx), (fy, cy) = EDGE[side[0]], EDGE[side[1]]
+            field[:, fx : fx + cx, fy : fy + cy] = jnp.zeros((4, cx, cy, 32, 128), BF16)
 
     r, q = iota((128, 128), 0), iota((128, 128), 1)
     to_wire = jnp.where(q == (r % 8) * 16 + r // 8, 1.0, 0.0).astype(BF16)
@@ -141,11 +150,22 @@
 
     def w_copy(k):
         return pltpu.make_async_remote_copy(
-            src_ref=w_stage,
-            dst_ref=w_got.at[af],
+            src_ref=w_stage.at[core],
+            dst_ref=w_got.at[af, core],
             send_sem=w_send.at[k],
             recv_sem=w_recv.at[k],
             device_id={"af": af_peer[k]},
+            device_id_type=MESH,
+        )
+
+    def pass_copy(k):
+        origin = (af + 4 - k) % 4
+        return pltpu.make_async_remote_copy(
+            src_ref=w_got.at[origin, core],
+            dst_ref=w_got.at[origin, core],
+            send_sem=pass_send.at[k],
+            recv_sem=pass_recv.at[k],
+            device_id={"gx": 2 * row + 1 - core},
             device_id_type=MESH,
         )
 
@@ -180,6 +200,8 @@
         w_copy(k).start()
     stage_input(COT, cot)
     for k in (2, 1, 3):
+        in_copy(VOL, k).wait_send()
+    for k in (2, 1, 3):
         in_copy(COT, k).start()
 
     def halo_copy(which, side):
@@ -224,6 +246,9 @@
 
     for k in range(1, 4):
         w_copy(k).wait_recv()
+        pass_copy(k).start()
+    for k in range(1, 4):
+        pass_copy(k).wait_recv()
 
     def taps_of(which):
         parts = [w_got[s, which].astype(F32) for s in range(4)]
@@ -333,14 +358,21 @@
                 window(COT, x, dx), own_hid, along, preferred_element_type=F32
             )
     bias_own = jnp.sum(bias_sum, axis=1, keepdims=True)
-    for dx in range(3):
-        for k in range(3):
-            for s in range(4):
-                rows = slice(32 * k + 8 * s, 32 * k + 8 * s + 8)
-                grad[0, s, 3 * dx + k, :, 0:96] = acc_one[dx][rows]
-                grad[1, s, 3 * dx + k, :, 0:96] = acc_two[dx][rows]
-    for s in range(4):
-        grad[0, s, 0, :, 96:97] = bias_own[8 * s : 8 * s + 8]
+    for which, acc in enumerate((acc_one, acc_two)):
+        for s in range(4):
+            blocks = [acc[k // 3][32 * (k % 3) + 8 * s : 32 * (k % 3) + 8 * s + 8] for k in range(9)]
+            tiles = []
+            for k in range(6):
+                cut = blocks[6 + k // 3][:, 32 * (k % 3) : 32 * (k % 3) + 32]
+                tiles.append(jnp.concatenate([blocks[k], cut], axis=1))
+            if which == 0:
+                extra = jnp.broadcast_to(bias_own[8 * s : 8 * s + 8], (8, 32))
+            else:
+                extra = jnp.zeros((8, 32), F32)
+            tiles.append(jnp.concatenate([blocks[8], extra], axis=1))
+            tiles.append(jnp.zeros((8, 128), F32))
+            for k in range(8):
+                grad[which, 4 * s + k // 2, k % 2] = tiles[k]
 
     core_copy = pltpu.make_async_remote_copy(
         src_ref=grad.at[1 - core],
@@ -378,68 +410,55 @@
 
     core_copy.wait_recv()
     core_sum[...] = grad[core] + core_got[...]
-    z_got[af] = core_sum[af]
-
-    def z_copy(k):
-        return pltpu.make_async_remote_copy(
-            src_ref=core_sum.at[af_peer[k]],
-            dst_ref=z_got.at[af],
-            send_sem=z_send.at[k],
-            recv_sem=z_recv.at[k],
-            device_id={"af": af_peer[k]},
-            device_id_type=MESH,
-        )
-
-    for k in range(1, 4):
-        z_copy(k).start()
+    plane_got[place] = core_sum[pl.ds(place * kept, kept)]
+
+    def plane_copy(k):
+        other_row, other_gy = at_place(k)
+        return pltpu.make_async_remote_copy(
+            src_ref=core_sum.at[pl.ds(((place + k) % plane) * kept, kept)],
+            dst_ref=plane_got.at[place],
+            send_sem=plane_send.at[k],
+            recv_sem=plane_recv.at[k],
+            device_id={"gx": 2 * other_row + core, "gy": other_gy},
+            device_id_type=MESH,
+        )
+
+    for k in range(1, plane):
+        plane_copy(k).start()
 
     halo_wait(PRE)
     produce(1, PRE, 1)
 
-    for k in range(1, 4):
-        z_copy(k).wait_recv()
-    y_got[row] = z_got[0] + z_got[1] + z_got[2] + z_got[3]
-
-    def y_copy(k):
-        return pltpu.make_async_remote_copy(
-            src_ref=y_got.at[row],
-            dst_ref=y_got.at[row],
-            send_sem=y_send.at[k],
-            recv_sem=y_recv.at[k],
-            device_id={"gx": 2 * ((row + k) % n_y) + core},
-            device_id_type=MESH,
-        )
-
-    for k in range(1, n_y):
-        y_copy(k).start()
-    for k in range(1, n_y):
-        y_copy(k).wait_recv()
-    x_got[col] = sum([y_got[i] for i in range(1, n_y)], y_got[0])
-
-    def x_copy(k):
-        return pltpu.make_async_remote_copy(
-            src_ref=x_got.at[col],
-            dst_ref=x_got.at[col],
-            send_sem=x_send.at[k],
-            recv_sem=x_recv.at[k],
-            device_id={"gy": high * n_x + (col + k) % n_x},
-            device_id_type=MESH,
-        )
-
-    for k in range(1, n_x):
-        x_copy(k).start()
-    for k in range(1, n_x):
-        x_copy(k).wait_recv()
-    h_stage[...] = sum([x_got[i] for i in range(1, n_x)], x_got[0])
-    h_copy = pltpu.make_async_remote_copy(
-        src_ref=h_stage,
-        dst_ref=h_got,
-        send_sem=h_send.at[0],
-        recv_sem=h_recv.at[0],
-        device_id={"gy": (1 - high) * n_x + col},
-        device_id_type=MESH,
-    )
-    h_copy.start()
+    for k in range(1, plane):
+        plane_copy(k).wait_recv()
+    line_stage[...] = sum([plane_got[i] for i in range(1, plane)], plane_got[0])
+
+    owner = (place * kept) // 4
+    mine = af == owner
+    at_line = high * 4 + af
+
+    def line_copy(half):
+        return pltpu.make_async_remote_copy(
+            src_ref=line_stage,
+            dst_ref=line_got.at[at_line],
+            send_sem=line_send.at[half],
+            recv_sem=line_recv.at[at_line],
+            device_id={"gy": half * n_x + col, "af": owner},
+            device_id_type=MESH,
+        )
+
+    def not_here(half):
+        return jnp.logical_not(jnp.logical_and(mine, high == half))
+
+    for half in range(2):
+
+        @pl.when(not_here(half))
+        def _(half=half):
+            line_copy(half).start()
+
+    @pl.when(mine)
+    def _():
+        line_got[at_line] = line_stage[...]
 
     def finish(which, target):
         for k in range(1, 4):
@@ -457,39 +476,85 @@
 
     finish(0, out)
     stores[0].start()
-    h_copy.wait_recv()
     scale = 1.0 / math.sqrt(4 * n_gx * 16 * n_gy * 128)
-    final[core] = (h_stage[...] + h_got[...]) * scale
-    last_copy = pltpu.make_async_remote_copy(
-        src_ref=final.at[core],
-        dst_ref=final.at[core],
-        send_sem=core_send.at[1],
-        recv_sem=core_recv.at[1],
-        device_id={"gx": 2 * row + 1 - core},
-        device_id_type=MESH,
-    )
-    last_copy.start()
+    quarter = (place * kept) % 4
+
+    def last_copy(k, same):
+        other_row, other_gy = at_place(k)
+        return pltpu.make_async_remote_copy(
+            src_ref=final.at[core, pl.ds(quarter, kept)],
+            dst_ref=final.at[core, pl.ds(quarter, kept)],
+            send_sem=last_send.at[2 * k + same],
+            recv_sem=last_recv.at[core, quarter],
+            device_id={"gx": 2 * other_row + (core if same else 1 - core), "gy": other_gy},
+            device_id_type=MESH,
+        )
+
+    @pl.when(mine)
+    def _():
+        for i in range(8):
+
+            @pl.when(at_line != i)
+            def _(i=i):
+                pltpu.make_async_remote_copy(
+                    src_ref=line_stage,
+                    dst_ref=line_got.at[i],
+                    send_sem=line_send.at[0],
+                    recv_sem=line_recv.at[i],
+                    device_id={"af": af_peer[1]},
+                    device_id_type=MESH,
+                ).wait_recv()
+
+        total = sum([line_got[i] for i in range(1, 8)], line_got[0])
+        final[core, pl.ds(quarter, kept)] = total * scale
+        for k in range(plane):
+            for same in (0, 1):
+                if k > 0 or same == 0:
+                    last_copy(k, same).start()
+
     finish(1, in_grad)
     stores[1].start()
-    last_copy.wait_recv()
-    for dx in range(3):
-        for k in range(3):
-            tile_one = final[0, 3 * dx + k]
-            tile_two = final[1, 3 * dx + k]
-            for m in range(3):
-                g_one[dx, m, k] = tile_one[:, 32 * m : 32 * m + 32]
-                g_two[2 - dx, 2 - k, m] = tile_two[:, 32 * m : 32 * m + 32]
-    g_bias[...] = jnp.sum(jnp.where(diag, final[0, 0][:, 96:97], 0.0), axis=0, keepdims=True)
+
+    for kind in range(2):
+        for part in range(0, 4, min(kept, 4)):
+
+            @pl.when(jnp.logical_not(jnp.logical_and(mine, jnp.logical_and(core == kind, quarter == part))))
+            def _(kind=kind, part=part):
+                pltpu.make_async_remote_copy(
+                    src_ref=final.at[kind, pl.ds(part, kept)],
+                    dst_ref=final.at[kind, pl.ds(part, kept)],
+                    send_sem=last_send.at[0],
+                    recv_sem=last_recv.at[kind, part],
+                    device_id={"gx": 2 * row + 1 - core},
+                    device_id_type=MESH,
+                ).wait_recv()
+
+    for kind in range(2):
+        tiles = [final[kind, k // 2, k % 2] for k in range(7)]
+        for a in range(3):
+            for b in range(3):
+                for c in range(3):
+                    k = 3 * a + b
+                    if k < 6:
+                        tap = tiles[k][:, 32 * c : 32 * c + 32]
+                    elif k < 8:
+                        tap = tiles[3 * (k - 6) + c][:, 96:128]
+                    else:
+                        tap = tiles[6][:, 32 * c : 32 * c + 32]
+                    if kind == 0:
+                        g_one[a, c, b] = tap
+                    else:
+                        g_two[2 - a, 2 - b, c] = tap
+    g_bias[...] = jnp.sum(jnp.where(diag, final[0, 3, 0][:, 96:97], 0.0), axis=0, keepdims=True)
     for copy in stores[2:]:
         copy.start()
 
     for k in range(1, 4):
-        in_copy(VOL, k).wait_send()
         in_copy(COT, k).wait_send()
         w_copy(k).wait_send()
         out_copy(0, k).wait_send()
         out_copy(1, k).wait_send()
-        z_copy(k).wait_send()
+        pass_copy(k).wait_send()
     for which in (VOL, COT, HID, PRE):
         for side in SIDES:
 
@@ -498,30 +563,40 @@
                 halo_copy(which, side).wait_send()
 
     core_copy.wait_send()
-    for k in range(1, n_y):
-        y_copy(k).wait_send()
-    for k in range(1, n_x):
-        x_copy(k).wait_send()
-    h_copy.wait_send()
-    last_copy.wait_send()
+    for k in range(1, plane):
+        plane_copy(k).wait_send()
+    for half in range(2):
+
+        @pl.when(not_here(half))
+        def _(half=half):
+            line_copy(half).wait_send()
+
+    @pl.when(mine)
+    def _():
+        for k in range(plane):
+            for same in (0, 1):
+                if k > 0 or same == 0:
+                    last_copy(k, same).wait_send()
+
     for copy in stores:
         copy.wait()
 
 
 def store(*refs):
-    sources, targets, sems = refs[:5], refs[5:10], refs[10]
-    copies = [
-        pltpu.make_async_copy(source, target, sems.at[i])
-        for i, (source, target) in enumerate(zip(sources, targets))
-    ]
-    for copy in copies:
+    sources, targets, held, sems = refs[:5], refs[5:10], refs[10:15], refs[15]
+    loads = [pltpu.make_async_copy(sources[i], held[i], sems.at[0, i]) for i in range(5)]
+    copies = [pltpu.make_async_copy(held[i], targets[i], sems.at[1, i]) for i in range(5)]
+    for load in loads:
+        load.start()
+    for load, copy in zip(loads, copies):
+        load.wait()
         copy.start()
     for copy in copies:
         copy.wait()
 
 
 def body(dims, volume, weight_one, bias_one, weight_two, cotangent):
-    n_y, n_x = dims[0] // 2, dims[1] // 2
+    plane = (dims[0] // 2) * (dims[1] // 2)
     as_taps = (2, 3, 4, 0, 1)
     dma = pltpu.SemaphoreType.DMA
     out, in_grad, g_one, g_bias, g_two = pl.pallas_call(
@@ -555,17 +630,16 @@
             pltpu.VMEM((4, 96, 288), BF16),
             pltpu.VMEM((2, 4, 4, 2, 16, 128), BF16),
             pltpu.VMEM((2, 4, 4, 2, 16, 128), BF16),
-            pltpu.VMEM((2, 4, 9, 8, 128), F32),
-            pltpu.VMEM((4, 9, 8, 128), F32),
-            pltpu.VMEM((4, 9, 8, 128), F32),
-            pltpu.VMEM((4, 9, 8, 128), F32),
-            pltpu.VMEM((n_y, 9, 8, 128), F32),
-            pltpu.VMEM((n_x, 9, 8, 128), F32),
-            pltpu.VMEM((9, 8, 128), F32),
-            pltpu.VMEM((9, 8, 128), F32),
-            pltpu.VMEM((2, 9, 8, 128), F32),
-            dma((2, 4)), dma((2, 4)), dma((4,)), dma((4,)), dma((4, 8)), dma((4, 8)), dma((2, 4)), dma((2, 4)),
-            dma((2,)), dma((2,)), dma((4,)), dma((4,)), dma((4,)), dma((4,)), dma((4,)), dma((4,)), dma((1,)), dma((1,)),
+            pltpu.VMEM((2, 16, 2, 8, 128), F32),
+            pltpu.VMEM((16, 2, 8, 128), F32),
+            pltpu.VMEM((16, 2, 8, 128), F32),
+            pltpu.VMEM((plane, 16 // plane, 2, 8, 128), F32),
+            pltpu.VMEM((16 // plane, 2, 8, 128), F32),
+            pltpu.VMEM((8, 16 // plane, 2, 8, 128), F32),
+            pltpu.VMEM((2, 4, 2, 8, 128), F32),
+            dma((2, 4)), dma((2, 4)), dma((4,)), dma((4,)), dma((4,)), dma((4,)),
+            dma((4, 8)), dma((4, 8)), dma((2, 4)), dma((2, 4)),
+            dma((1,)), dma((1,)), dma((plane,)), dma((plane,)), dma((2,)), dma((8,)), dma((2 * plane,)), dma((2, 4)),
             dma((5,)), dma((5,)),
         ],
         compiler_params=pltpu.CompilerParams(
@@ -584,7 +658,7 @@
         out_shape=tuple(jax.ShapeDtypeStruct(part.shape, part.dtype) for part in results),
         in_specs=[pl.BlockSpec(memory_space=pltpu.HBM)] * 5,
         out_specs=[pl.BlockSpec(memory_space=pltpu.HBM)] * 5,
-        scratch_shapes=[dma((5,))],
+        scratch_shapes=[pltpu.VMEM(part.shape, part.dtype) for part in results] + [dma((2, 5))],
         compiler_params=pltpu.CompilerParams(vmem_limit_bytes=60 * 1024 * 1024),
     )(*results)
     as_given = (3, 4, 0, 1, 2)

time: 70.2 us -> 49.7 us (0.71)
  Pallas kernels: 69.5 us -> 49 us
    pallas_call x1, Pallas kernels: 15.8 us -> 1.81 us  [body(): pl.pallas_call(store, out_shape=tuple((jax.ShapeDtypeStruct(part.shape, p...]
    pallas_call x1, Pallas kernels: 53.7 us -> 47.2 us  [body(): pl.pallas_call(functools.partial(kernel, dims), out_shape=(jax.ShapeDtype...]
where the time goes in v3:
time: 49.7 us; the launch traced here: 49.6 us
  Pallas kernels  49 us (99%)
  between operations  0.64 us (1%)
    pallas_call x1, Pallas kernels, body(): pl.pallas_call(functools.partial(kernel, dims), out_shape=(jax.ShapeDtype...  47.2 us
    pallas_call x1, Pallas kernels, body(): pl.pallas_call(store, out_shape=tuple((jax.ShapeDtypeStruct(part.shape, p...  1.81 us

profile of v3, /device:TPU:1, one launch (start us, length us, event | category | flops | bytes accessed | tf_op | source)
XLA Modules:
  0.0 49.6 jit_solution(15008764101187964603)
XLA Ops:
  0.6 47.2 %shard_map.92 = (bf16[8,4,16,128]{3,2,1,0:T(8,128)(2,1)}, bf16[8,4,16,128]{3,2,1,0:T(8,128)(2,1)}, f32[3,3,3,8,32]{4,3,2,1,0:T(8,128)}, f32[1,8]{1,0:T(1,128)}, f32[3,3,3,8,32]{4,3,2,1,0:T(8,128)}) custom-call(bf16[8,4,16,128]{3,2,1,0:T(8,128)(2,1)} %vol_in.1, bf16[3,3,3,8,32]{4,3,2,1,0:T(8,128)(2,1)} %bitcast.6, f32[1,8]{1,0:T(1,128)} %bitcast.8, ...), custom_call_target="tpu_custom_call" | custom-call | tf_op jit(solution)/shard_map/pallas_call | solution.py:602
  47.8 1.8 %shard_map.93 = (bf16[8,4,16,128]{3,2,1,0:T(8,128)(2,1)}, bf16[8,4,16,128]{3,2,1,0:T(8,128)(2,1)}, f32[3,3,3,8,32]{4,3,2,1,0:T(8,128)}, f32[1,8]{1,0:T(1,128)}, f32[3,3,3,8,32]{4,3,2,1,0:T(8,128)}) custom-call(bf16[8,4,16,128]{3,2,1,0:T(8,128)(2,1)} %get-tuple-element.15.refs_0_, bf16[8,4,16,128]{3,2,1,0:T(8,128)(2,1)} %get-tuple-element.16.refs_1_, ...), custom_call_target="tpu_custom_call" | custom-call | tf_op jit(solution)/shard_map/pallas_call | solution.py:656

commit v4 on v3

--- a/solution.py
+++ b/solution.py
@@ -32,7 +32,7 @@
     stage, got, w_stage, w_got, field, pre_act, lhs,
     out_stage, out_got, grad, core_got, core_sum, plane_got, line_stage, line_got, final,
     in_send, in_recv, w_send, w_recv, pass_send, pass_recv, halo_send, halo_recv, out_send, out_recv,
-    core_send, core_recv, plane_send, plane_recv, line_send, line_recv, last_send, last_recv, load_sem, store_sem,
+    core_send, core_recv, plane_send, plane_recv, line_send, line_recv, last_send, last_recv, load_sem, store_sem, line_in,
 ):
     loads = [
         pltpu.make_async_copy(source, target, load_sem.at[i])
@@ -101,14 +101,10 @@
         return other // n_x, high * n_x + other % n_x
 
     barrier = pltpu.get_barrier_semaphore()
-    partners = []
-    for k in range(plane):
-        other_row, other_gy = at_place(k)
-        for other_core in (1 - core, core):
-            partners.append({"gx": 2 * other_row + other_core, "gy": other_gy, "af": af})
-    partners.pop(1)
-    for k in range(1, 8):
-        partners.append({"gx": gx, "gy": ((high + k // 4) % 2) * n_x + col, "af": af_peer[k % 4]})
+    across = [{"gy": high * n_x + (col + k) % n_x} for k in range(1, n_x)]
+    across += [{"gy": (1 - high) * n_x + col}]
+    partners = across + [{"af": af_peer[k]} for k in range(1, 4)]
+    partners += [{"gx": 2 * ((row + k) % n_y) + core} for k in range(1, n_y)]
     for partner in partners:
         pl.semaphore_signal(barrier, inc=1, device_id=partner, device_id_type=MESH)
     expected = jnp.int32(len(partners))
@@ -174,6 +170,8 @@
     pl.semaphore_wait(barrier, expected)
     for k in (2, 1, 3):
         in_copy(VOL, k).start()
+    for partner in across:
+        pl.semaphore_signal(line_in, inc=1, device_id=partner, device_id_type=MESH)
 
     for load in loads[1:]:
         load.wait()
@@ -309,6 +307,10 @@
             lines.append(part[32:64] + shift_up(part[0:32]) + shift_down(part[64:96]))
         return lines
 
+    for k in range(1, 4):
+        in_copy(COT, k).wait_recv()
+    assemble(COT)
+    halo_start(COT)
     halo_wait(VOL)
     for x in range(4):
         for y, line in enumerate(conv(VOL, 0, x)):
@@ -317,10 +319,6 @@
             field[HID, 1 + x, 1 + y] = (act / (1.0 + jnp.exp(-act))).astype(BF16)
     halo_start(HID)
 
-    for k in range(1, 4):
-        in_copy(COT, k).wait_recv()
-    assemble(COT)
-    halo_start(COT)
     make_forward(1)
     make_turned(0)
     halo_wait(COT)
@@ -372,7 +370,8 @@
             tiles.append(jnp.concatenate([blocks[8], extra], axis=1))
             tiles.append(jnp.zeros((8, 128), F32))
             for k in range(8):
-                grad[which, 4 * s + k // 2, k % 2] = tiles[k]
+                grad[which, 2 * k, s] = tiles[k][0:4]
+                grad[which, 2 * k + 1, s] = tiles[k][4:8]
 
     core_copy = pltpu.make_async_remote_copy(
         src_ref=grad.at[1 - core],
@@ -408,6 +407,7 @@
     halo_wait(HID)
     produce(0, HID, 2)
 
+    pl.semaphore_wait(line_in, len(across))
     core_copy.wait_recv()
     core_sum[...] = grad[core] + core_got[...]
     plane_got[place] = core_sum[pl.ds(place * kept, kept)]
@@ -433,32 +433,22 @@
         plane_copy(k).wait_recv()
     line_stage[...] = sum([plane_got[i] for i in range(1, plane)], plane_got[0])
 
-    owner = (place * kept) // 4
-    mine = af == owner
     at_line = high * 4 + af
-
-    def line_copy(half):
-        return pltpu.make_async_remote_copy(
-            src_ref=line_stage,
+    line_got[at_line] = line_stage[:, pl.ds(af, 1)].reshape(kept, 4, 128)
+
+    def line_copy(k):
+        other = af_peer[k % 4]
+        return pltpu.make_async_remote_copy(
+            src_ref=line_stage.at[:, other],
             dst_ref=line_got.at[at_line],
-            send_sem=line_send.at[half],
-            recv_sem=line_recv.at[at_line],
-            device_id={"gy": half * n_x + col, "af": owner},
-            device_id_type=MESH,
-        )
-
-    def not_here(half):
-        return jnp.logical_not(jnp.logical_and(mine, high == half))
-
-    for half in range(2):
-
-        @pl.when(not_here(half))
-        def _(half=half):
-            line_copy(half).start()
-
-    @pl.when(mine)
-    def _():
-        line_got[at_line] = line_stage[...]
+            send_sem=line_send.at[k],
+            recv_sem=line_recv.at[k],
+            device_id={"gy": ((high + k // 4) % 2) * n_x + col, "af": other},
+            device_id_type=MESH,
+        )
+
+    for k in range(1, 8):
+        line_copy(k).start()
 
     def finish(which, target):
         for k in range(1, 4):
@@ -477,60 +467,37 @@
     finish(0, out)
     stores[0].start()
     scale = 1.0 / math.sqrt(4 * n_gx * 16 * n_gy * 128)
-    quarter = (place * kept) % 4
 
     def last_copy(k, same):
         other_row, other_gy = at_place(k)
-        return pltpu.make_async_remote_copy(
-            src_ref=final.at[core, pl.ds(quarter, kept)],
-            dst_ref=final.at[core, pl.ds(quarter, kept)],
+        part = final.at[core, pl.ds(place * kept, kept)]
+        return pltpu.make_async_remote_copy(
+            src_ref=part,
+            dst_ref=part,
             send_sem=last_send.at[2 * k + same],
-            recv_sem=last_recv.at[core, quarter],
+            recv_sem=last_recv.at[2 * k + same],
             device_id={"gx": 2 * other_row + (core if same else 1 - core), "gy": other_gy},
             device_id_type=MESH,
         )
 
-    @pl.when(mine)
-    def _():
-        for i in range(8):
-
-            @pl.when(at_line != i)
-            def _(i=i):
-                pltpu.make_async_remote_copy(
-                    src_ref=line_stage,
-                    dst_ref=line_got.at[i],
-                    send_sem=line_send.at[0],
-                    recv_sem=line_recv.at[i],
-                    device_id={"af": af_peer[1]},
-                    device_id_type=MESH,
-                ).wait_recv()
-
-        total = sum([line_got[i] for i in range(1, 8)], line_got[0])
-        final[core, pl.ds(quarter, kept)] = total * scale
-        for k in range(plane):
-            for same in (0, 1):
-                if k > 0 or same == 0:
-                    last_copy(k, same).start()
+    others = [(k, same) for k in range(plane) for same in (1, 0)][1:]
+    for k in range(1, 8):
+        line_copy(k).wait_recv()
+    total = sum([line_got[i] for i in range(1, 8)], line_got[0])
+    final[core, pl.ds(place * kept, kept)] = total * scale
+    for k, same in others:
+        last_copy(k, same).start()
 
     finish(1, in_grad)
     stores[1].start()
 
+    for k, same in others:
+        last_copy(k, same).wait_recv()
+
     for kind in range(2):
-        for part in range(0, 4, min(kept, 4)):
-
-            @pl.when(jnp.logical_not(jnp.logical_and(mine, jnp.logical_and(core == kind, quarter == part))))
-            def _(kind=kind, part=part):
-                pltpu.make_async_remote_copy(
-                    src_ref=final.at[kind, pl.ds(part, kept)],
-                    dst_ref=final.at[kind, pl.ds(part, kept)],
-                    send_sem=last_send.at[0],
-                    recv_sem=last_recv.at[kind, part],
-                    device_id={"gx": 2 * row + 1 - core},
-                    device_id_type=MESH,
-                ).wait_recv()
-
-    for kind in range(2):
-        tiles = [final[kind, k // 2, k % 2] for k in range(7)]
+        tiles = [jnp.concatenate([final[kind, 2 * k], final[kind, 2 * k + 1]], axis=0) for k in range(7)]
+        if kind == 0:
+            bias_total = tiles[6][:, 96:97]
         for a in range(3):
             for b in range(3):
                 for c in range(3):
@@ -545,7 +512,7 @@
                         g_one[a, c, b] = tap
                     else:
                         g_two[2 - a, 2 - b, c] = tap
-    g_bias[...] = jnp.sum(jnp.where(diag, final[0, 3, 0][:, 96:97], 0.0), axis=0, keepdims=True)
+    g_bias[...] = jnp.sum(jnp.where(diag, bias_total, 0.0), axis=0, keepdims=True)
     for copy in stores[2:]:
         copy.start()
 
@@ -565,19 +532,10 @@
     core_copy.wait_send()
     for k in range(1, plane):
         plane_copy(k).wait_send()
-    for half in range(2):
-
-        @pl.when(not_here(half))
-        def _(half=half):
-            line_copy(half).wait_send()
-
-    @pl.when(mine)
-    def _():
-        for k in range(plane):
-            for same in (0, 1):
-                if k > 0 or same == 0:
-                    last_copy(k, same).wait_send()
-
+    for k in range(1, 8):
+        line_copy(k).wait_send()
+    for k, same in others:
+        last_copy(k, same).wait_send()
     for copy in stores:
         copy.wait()
 
@@ -630,17 +588,17 @@
             pltpu.VMEM((4, 96, 288), BF16),
             pltpu.VMEM((2, 4, 4, 2, 16, 128), BF16),
             pltpu.VMEM((2, 4, 4, 2, 16, 128), BF16),
-            pltpu.VMEM((2, 16, 2, 8, 128), F32),
-            pltpu.VMEM((16, 2, 8, 128), F32),
-            pltpu.VMEM((16, 2, 8, 128), F32),
-            pltpu.VMEM((plane, 16 // plane, 2, 8, 128), F32),
-            pltpu.VMEM((16 // plane, 2, 8, 128), F32),
-            pltpu.VMEM((8, 16 // plane, 2, 8, 128), F32),
-            pltpu.VMEM((2, 4, 2, 8, 128), F32),
+            pltpu.VMEM((2, 16, 4, 4, 128), F32),
+            pltpu.VMEM((16, 4, 4, 128), F32),
+            pltpu.VMEM((16, 4, 4, 128), F32),
+            pltpu.VMEM((plane, 16 // plane, 4, 4, 128), F32),
+            pltpu.VMEM((16 // plane, 4, 4, 128), F32),
+            pltpu.VMEM((8, 16 // plane, 4, 128), F32),
+            pltpu.VMEM((2, 16, 4, 128), F32),
             dma((2, 4)), dma((2, 4)), dma((4,)), dma((4,)), dma((4,)), dma((4,)),
             dma((4, 8)), dma((4, 8)), dma((2, 4)), dma((2, 4)),
-            dma((1,)), dma((1,)), dma((plane,)), dma((plane,)), dma((2,)), dma((8,)), dma((2 * plane,)), dma((2, 4)),
-            dma((5,)), dma((5,)),
+            dma((1,)), dma((1,)), dma((plane,)), dma((plane,)), dma((8,)), dma((8,)), dma((2 * plane,)), dma((2 * plane,)),
+            dma((5,)), dma((5,)), pltpu.SemaphoreType.REGULAR,
         ],
         compiler_params=pltpu.CompilerParams(
             collective_id=0, has_side_effects=True, vmem_limit_bytes=60 * 1024 * 1024

time: 49.7 us -> 47.2 us (0.950)
  Pallas kernels: 49 us -> 46.4 us
    pallas_call x1, Pallas kernels: 47.2 us -> 44.6 us  [body(): pl.pallas_call(functools.partial(kernel, dims), out_shape=(jax.ShapeDtype...]
where the time goes in v4:
time: 47.2 us; the launch traced here: 47.1 us
  Pallas kernels  46.4 us (98%)
  between operations  0.64 us (1%)
    pallas_call x1, Pallas kernels, body(): pl.pallas_call(functools.partial(kernel, dims), out_shape=(jax.ShapeDtype...  44.6 us
    pallas_call x1, Pallas kernels, body(): pl.pallas_call(store, out_shape=tuple((jax.ShapeDtypeStruct(part.shape, p...  1.81 us

profile of v4, /device:TPU:1, one launch (start us, length us, event | category | flops | bytes accessed | tf_op | source)
XLA Modules:
  0.0 47.1 jit_solution(6338837551929758236)
XLA Ops:
  0.6 44.6 %shard_map.92 = (bf16[8,4,16,128]{3,2,1,0:T(8,128)(2,1)}, bf16[8,4,16,128]{3,2,1,0:T(8,128)(2,1)}, f32[3,3,3,8,32]{4,3,2,1,0:T(8,128)}, f32[1,8]{1,0:T(1,128)}, f32[3,3,3,8,32]{4,3,2,1,0:T(8,128)}) custom-call(bf16[8,4,16,128]{3,2,1,0:T(8,128)(2,1)} %vol_in.1, bf16[3,3,3,8,32]{4,3,2,1,0:T(8,128)(2,1)} %bitcast.6, f32[1,8]{1,0:T(1,128)} %bitcast.8, ...), custom_call_target="tpu_custom_call" | custom-call | tf_op jit(solution)/shard_map/pallas_call | solution.py:560
  45.2 1.8 %shard_map.93 = (bf16[8,4,16,128]{3,2,1,0:T(8,128)(2,1)}, bf16[8,4,16,128]{3,2,1,0:T(8,128)(2,1)}, f32[3,3,3,8,32]{4,3,2,1,0:T(8,128)}, f32[1,8]{1,0:T(1,128)}, f32[3,3,3,8,32]{4,3,2,1,0:T(8,128)}) custom-call(bf16[8,4,16,128]{3,2,1,0:T(8,128)(2,1)} %get-tuple-element.15.refs_0_, bf16[8,4,16,128]{3,2,1,0:T(8,128)(2,1)} %get-tuple-element.16.refs_1_, ...), custom_call_target="tpu_custom_call" | custom-call | tf_op jit(solution)/shard_map/pallas_call | solution.py:614

commit v5 on v4

--- a/solution.py
+++ b/solution.py
@@ -13,7 +13,8 @@
 BF16 = jnp.bfloat16
 
 VOL, COT, HID, PRE = 0, 1, 2, 3
-SIDES = [(dx, dy) for dx in (-1, 0, 1) for dy in (-1, 0, 1) if (dx, dy) != (0, 0)]
+SIDES = [(-1, -1), (-1, 1), (1, -1), (1, 1), (0, -1), (0, 1), (-1, 0), (1, 0)]
+FAR = (10, 9, 11, 6, 14, 8, 2, 5, 7, 13, 15, 1, 3, 4, 12)
 SEND = {-1: (1, 1), 0: (1, 4), 1: (4, 1)}
 EDGE = {-1: (0, 1), 0: (1, 4), 1: (5, 1)}
 LAND = {-1: (5, 1), 0: (1, 4), 1: (0, 1)}
@@ -26,8 +27,8 @@
 def kernel(
     dims,
     vol_in, w_one_in, bias_in, w_two_in, cot_in,
-    out_to, in_grad_to, g_one_to, g_bias_to, g_two_to,
-    out, in_grad, g_one, g_bias, g_two,
+    out_to, in_grad_to, final_to,
+    out, in_grad,
     vol, w_one, bias, w_two, cot,
     stage, got, w_stage, w_got, field, pre_act, lhs,
     out_stage, out_got, grad, core_got, core_sum, plane_got, line_stage, line_got, final,
@@ -45,7 +46,7 @@
     stores = [
         pltpu.make_async_copy(source, target, store_sem.at[i])
         for i, (source, target) in enumerate(
-            ((out, out_to), (in_grad, in_grad_to), (g_one, g_one_to), (g_bias, g_bias_to), (g_two, g_two_to))
+            ((out, out_to), (in_grad, in_grad_to), (final, final_to))
         )
     ]
     n_gx, n_gy = dims
@@ -68,7 +69,7 @@
         if step == 0:
             return gy, af
         inside = (sub < 3) if step > 0 else (sub > 0)
-        gy_new = jnp.where(inside, gy, gy + step)
+        gy_new = jnp.where(inside, gy, (gy + step + n_gy) % n_gy)
         sub_new = jnp.where(inside, sub + step, 0 if step > 0 else 3)
         return gy_new, sub_of(sub_new, gy_new)
 
@@ -86,40 +87,32 @@
             return checks[0]
         return jnp.logical_and(checks[0], checks[1])
 
-    neighbour = {}
-    for dx, dy in SIDES:
-        gy_new, af_new = y_neighbour(dy)
-        neighbour[dx, dy] = {"gx": gx + dx, "gy": gy_new, "af": af_new}
+    ring = {step: y_neighbour(step) for step in (-1, 0, 1)}
+    neighbour = {(dx, dy): {"gx": gx + dx, "gy": ring[dy][0], "af": ring[dy][1]} for dx, dy in SIDES}
     af_peer = [(af + k) % 4 for k in range(4)]
 
     plane = n_y * n_x
     place = row * n_x + col
     kept = 16 // plane
+    far = [k for k in FAR if k < plane]
 
     def at_place(k):
         other = (place + k) % plane
         return other // n_x, high * n_x + other % n_x
+
+    for side in SIDES:
+        (fx, cx), (fy, cy) = EDGE[side[0]], EDGE[side[1]]
+        field[:, fx : fx + cx, fy : fy + cy] = jnp.zeros((4, cx, cy, 32, 128), BF16)
 
     barrier = pltpu.get_barrier_semaphore()
     across = [{"gy": high * n_x + (col + k) % n_x} for k in range(1, n_x)]
     across += [{"gy": (1 - high) * n_x + col}]
     partners = across + [{"af": af_peer[k]} for k in range(1, 4)]
     partners += [{"gx": 2 * ((row + k) % n_y) + core} for k in range(1, n_y)]
+    for dx, dy in SIDES:
+        partners.append({"gx": (gx + dx + n_gx) % n_gx, "gy": ring[dy][0], "af": ring[dy][1]})
     for partner in partners:
         pl.semaphore_signal(barrier, inc=1, device_id=partner, device_id_type=MESH)
-    expected = jnp.int32(len(partners))
-    for side in SIDES:
-
-        @pl.when(has(*side))
-        def _(side=side):
-            pl.semaphore_signal(barrier, inc=1, device_id=neighbour[side], device_id_type=MESH)
-
-        expected = expected + has(*side).astype(jnp.int32)
-
-        @pl.when(jnp.logical_not(has(*side)))
-        def _(side=side):
-            (fx, cx), (fy, cy) = EDGE[side[0]], EDGE[side[1]]
-            field[:, fx : fx + cx, fy : fy + cy] = jnp.zeros((4, cx, cy, 32, 128), BF16)
 
     r, q = iota((128, 128), 0), iota((128, 128), 1)
     to_wire = jnp.where(q == (r % 8) * 16 + r // 8, 1.0, 0.0).astype(BF16)
@@ -167,12 +160,6 @@
 
     loads[0].wait()
     stage_input(VOL, vol)
-    pl.semaphore_wait(barrier, expected)
-    for k in (2, 1, 3):
-        in_copy(VOL, k).start()
-    for partner in across:
-        pl.semaphore_signal(line_in, inc=1, device_id=partner, device_id_type=MESH)
-
     for load in loads[1:]:
         load.wait()
     diag = iota((8, 8), 0) == iota((8, 8), 1)
@@ -194,6 +181,12 @@
         packed = jnp.concatenate(groups, axis=0).astype(BF16)
         w_stage[which] = packed
         w_got[af, which] = packed
+    pl.semaphore_wait(barrier, len(partners))
+    for k in (2, 1, 3):
+        in_copy(VOL, k).start()
+    for partner in across:
+        pl.semaphore_signal(line_in, inc=1, device_id=partner, device_id_type=MESH)
+
     for k in (2, 1, 3):
         w_copy(k).start()
     stage_input(COT, cot)
@@ -245,6 +238,10 @@
     for k in range(1, 4):
         w_copy(k).wait_recv()
         pass_copy(k).start()
+    for k in range(1, 4):
+        in_copy(COT, k).wait_recv()
+    assemble(COT)
+    halo_start(COT)
     for k in range(1, 4):
         pass_copy(k).wait_recv()
 
@@ -307,10 +304,6 @@
             lines.append(part[32:64] + shift_up(part[0:32]) + shift_down(part[64:96]))
         return lines
 
-    for k in range(1, 4):
-        in_copy(COT, k).wait_recv()
-    assemble(COT)
-    halo_start(COT)
     halo_wait(VOL)
     for x in range(4):
         for y, line in enumerate(conv(VOL, 0, x)):
@@ -423,7 +416,7 @@
             device_id_type=MESH,
         )
 
-    for k in range(1, plane):
+    for k in far:
         plane_copy(k).start()
 
     halo_wait(PRE)
@@ -434,21 +427,26 @@
     line_stage[...] = sum([plane_got[i] for i in range(1, plane)], plane_got[0])
 
     at_line = high * 4 + af
-    line_got[at_line] = line_stage[:, pl.ds(af, 1)].reshape(kept, 4, 128)
-
-    def line_copy(k):
+    line_got[core, at_line] = line_stage[:, pl.ds(af, 1)].reshape(kept, 4, 128)
+
+    def line_copy(k, same):
         other = af_peer[k % 4]
         return pltpu.make_async_remote_copy(
             src_ref=line_stage.at[:, other],
-            dst_ref=line_got.at[at_line],
-            send_sem=line_send.at[k],
-            recv_sem=line_recv.at[k],
-            device_id={"gy": ((high + k // 4) % 2) * n_x + col, "af": other},
-            device_id_type=MESH,
-        )
-
-    for k in range(1, 8):
-        line_copy(k).start()
+            dst_ref=line_got.at[core, at_line],
+            send_sem=line_send.at[2 * k + same],
+            recv_sem=line_recv.at[2 * k + same],
+            device_id={
+                "gx": 2 * row + (core if same else 1 - core),
+                "gy": ((high + k // 4) % 2) * n_x + col,
+                "af": other,
+            },
+            device_id_type=MESH,
+        )
+
+    line_others = [(k, same) for k in (4, 5, 6, 7, 2, 3, 1) for same in (1, 0)] + [(0, 0)]
+    for k, same in line_others:
+        line_copy(k, same).start()
 
     def finish(which, target):
         for k in range(1, 4):
@@ -468,34 +466,79 @@
     stores[0].start()
     scale = 1.0 / math.sqrt(4 * n_gx * 16 * n_gy * 128)
 
-    def last_copy(k, same):
+    def last_copy(k):
         other_row, other_gy = at_place(k)
-        part = final.at[core, pl.ds(place * kept, kept)]
+        part = final.at[place]
         return pltpu.make_async_remote_copy(
             src_ref=part,
             dst_ref=part,
-            send_sem=last_send.at[2 * k + same],
-            recv_sem=last_recv.at[2 * k + same],
-            device_id={"gx": 2 * other_row + (core if same else 1 - core), "gy": other_gy},
-            device_id_type=MESH,
-        )
-
-    others = [(k, same) for k in range(plane) for same in (1, 0)][1:]
-    for k in range(1, 8):
-        line_copy(k).wait_recv()
-    total = sum([line_got[i] for i in range(1, 8)], line_got[0])
-    final[core, pl.ds(place * kept, kept)] = total * scale
-    for k, same in others:
-        last_copy(k, same).start()
+            send_sem=last_send.at[k],
+            recv_sem=last_recv.at[k],
+            device_id={"gx": 2 * other_row + core, "gy": other_gy},
+            device_id_type=MESH,
+        )
+
+    for k, same in line_others:
+        line_copy(k, same).wait_recv()
+    for kind in range(2):
+        total = sum([line_got[kind, i] for i in range(1, 8)], line_got[kind, 0])
+        final[place, pl.ds(kind * kept, kept)] = total * scale
+    for k in far:
+        last_copy(k).start()
 
     finish(1, in_grad)
     stores[1].start()
 
-    for k, same in others:
-        last_copy(k, same).wait_recv()
-
+    for k in range(1, plane):
+        last_copy(k).wait_recv()
+
+    stores[2].start()
+
+    for k in range(1, 4):
+        in_copy(COT, k).wait_send()
+        w_copy(k).wait_send()
+        out_copy(0, k).wait_send()
+        out_copy(1, k).wait_send()
+        pass_copy(k).wait_send()
+    for which in (VOL, COT, HID, PRE):
+        for side in SIDES:
+
+            @pl.when(has(*side))
+            def _(which=which, side=side):
+                halo_copy(which, side).wait_send()
+
+    core_copy.wait_send()
+    for k in range(1, plane):
+        plane_copy(k).wait_send()
+    for k, same in line_others:
+        line_copy(k, same).wait_send()
+    for k in range(1, plane):
+        last_copy(k).wait_send()
+    for copy in stores:
+        copy.wait()
+
+
+def store(
+    kept, out_in, in_grad_in, final_in, out_to, in_grad_to, g_one_to, g_bias_to, g_two_to,
+    out, in_grad, final, g_one, g_bias, g_two, sems,
+):
+    loads = [
+        pltpu.make_async_copy(source, target, sems.at[0, i])
+        for i, (source, target) in enumerate(((final_in, final), (out_in, out), (in_grad_in, in_grad)))
+    ]
+    stores = [
+        pltpu.make_async_copy(source, target, sems.at[1, i])
+        for i, (source, target) in enumerate(
+            ((out, out_to), (in_grad, in_grad_to), (g_one, g_one_to), (g_bias, g_bias_to), (g_two, g_two_to))
+        )
+    ]
+    for load in loads:
+        load.start()
+    loads[0].wait()
+    diag = iota((8, 8), 0) == iota((8, 8), 1)
     for kind in range(2):
-        tiles = [jnp.concatenate([final[kind, 2 * k], final[kind, 2 * k + 1]], axis=0) for k in range(7)]
+        halves = [final[k // kept, kind * kept + k % kept] for k in range(14)]
+        tiles = [jnp.concatenate(halves[2 * k : 2 * k + 2], axis=0) for k in range(7)]
         if kind == 0:
             bias_total = tiles[6][:, 96:97]
         for a in range(3):
@@ -515,41 +558,10 @@
     g_bias[...] = jnp.sum(jnp.where(diag, bias_total, 0.0), axis=0, keepdims=True)
     for copy in stores[2:]:
         copy.start()
-
-    for k in range(1, 4):
-        in_copy(COT, k).wait_send()
-        w_copy(k).wait_send()
-        out_copy(0, k).wait_send()
-        out_copy(1, k).wait_send()
-        pass_copy(k).wait_send()
-    for which in (VOL, COT, HID, PRE):
-        for side in SIDES:
-
-            @pl.when(has(*side))
-            def _(which=which, side=side):
-                halo_copy(which, side).wait_send()
-
-    core_copy.wait_send()
-    for k in range(1, plane):
-        plane_copy(k).wait_send()
-    for k in range(1, 8):
-        line_copy(k).wait_send()
-    for k, same in others:
-        last_copy(k, same).wait_send()
-    for copy in stores:
-        copy.wait()
-
-
-def store(*refs):
-    sources, targets, held, sems = refs[:5], refs[5:10], refs[10:15], refs[15]
-    loads = [pltpu.make_async_copy(sources[i], held[i], sems.at[0, i]) for i in range(5)]
-    copies = [pltpu.make_async_copy(held[i], targets[i], sems.at[1, i]) for i in range(5)]
-    for load in loads:
-        load.start()
-    for load, copy in zip(loads, copies):
+    for load, copy in zip(loads[1:], stores):
         load.wait()
         copy.start()
-    for copy in copies:
+    for copy in stores:
         copy.wait()
 
 
@@ -557,23 +569,17 @@
     plane = (dims[0] // 2) * (dims[1] // 2)
     as_taps = (2, 3, 4, 0, 1)
     dma = pltpu.SemaphoreType.DMA
-    out, in_grad, g_one, g_bias, g_two = pl.pallas_call(
+    cells = jax.ShapeDtypeStruct((8, 4, 16, 128), BF16)
+    taps = jax.ShapeDtypeStruct((3, 3, 3, 8, 32), F32)
+    dense = jax.ShapeDtypeStruct((plane, 2 * (16 // plane), 4, 128), F32)
+    results = pl.pallas_call(
         functools.partial(kernel, dims),
-        out_shape=(
-            jax.ShapeDtypeStruct((8, 4, 16, 128), BF16),
-            jax.ShapeDtypeStruct((8, 4, 16, 128), BF16),
-            jax.ShapeDtypeStruct((3, 3, 3, 8, 32), F32),
-            jax.ShapeDtypeStruct((1, 8), F32),
-            jax.ShapeDtypeStruct((3, 3, 3, 8, 32), F32),
-        ),
+        out_shape=(cells, cells, dense),
         in_specs=[pl.BlockSpec(memory_space=pltpu.HBM)] * 5,
-        out_specs=[pl.BlockSpec(memory_space=pltpu.HBM)] * 5,
+        out_specs=[pl.BlockSpec(memory_space=pltpu.HBM)] * 3,
         scratch_shapes=[
             pltpu.VMEM((8, 4, 16, 128), BF16),
             pltpu.VMEM((8, 4, 16, 128), BF16),
-            pltpu.VMEM((3, 3, 3, 8, 32), F32),
-            pltpu.VMEM((1, 8), F32),
-            pltpu.VMEM((3, 3, 3, 8, 32), F32),
             pltpu.VMEM((8, 4, 16, 128), BF16),
             pltpu.VMEM((3, 3, 3, 8, 32), BF16),
             pltpu.VMEM((1, 8), F32),
@@ -593,12 +599,12 @@
             pltpu.VMEM((16, 4, 4, 128), F32),
             pltpu.VMEM((plane, 16 // plane, 4, 4, 128), F32),
             pltpu.VMEM((16 // plane, 4, 4, 128), F32),
-            pltpu.VMEM((8, 16 // plane, 4, 128), F32),
-            pltpu.VMEM((2, 16, 4, 128), F32),
+            pltpu.VMEM((2, 8, 16 // plane, 4, 128), F32),
+            pltpu.VMEM((plane, 2 * (16 // plane), 4, 128), F32),
             dma((2, 4)), dma((2, 4)), dma((4,)), dma((4,)), dma((4,)), dma((4,)),
             dma((4, 8)), dma((4, 8)), dma((2, 4)), dma((2, 4)),
-            dma((1,)), dma((1,)), dma((plane,)), dma((plane,)), dma((8,)), dma((8,)), dma((2 * plane,)), dma((2 * plane,)),
-            dma((5,)), dma((5,)), pltpu.SemaphoreType.REGULAR,
+            dma((1,)), dma((1,)), dma((plane,)), dma((plane,)), dma((16,)), dma((16,)), dma((plane,)), dma((plane,)),
+            dma((5,)), dma((3,)), pltpu.SemaphoreType.REGULAR,
         ],
         compiler_params=pltpu.CompilerParams(
             collective_id=0, has_side_effects=True, vmem_limit_bytes=60 * 1024 * 1024
@@ -610,13 +616,14 @@
         jnp.transpose(weight_two, as_taps),
         cotangent,
     )
-    results = (out, in_grad, g_one, g_bias, g_two)
+    given = (cells, cells, taps, jax.ShapeDtypeStruct((1, 8), F32), taps)
     out, in_grad, g_one, g_bias, g_two = pl.pallas_call(
-        store,
-        out_shape=tuple(jax.ShapeDtypeStruct(part.shape, part.dtype) for part in results),
-        in_specs=[pl.BlockSpec(memory_space=pltpu.HBM)] * 5,
+        functools.partial(store, 16 // plane),
+        out_shape=given,
+        in_specs=[pl.BlockSpec(memory_space=pltpu.HBM)] * 3,
         out_specs=[pl.BlockSpec(memory_space=pltpu.HBM)] * 5,
-        scratch_shapes=[pltpu.VMEM(part.shape, part.dtype) for part in results] + [dma((2, 5))],
+        scratch_shapes=[pltpu.VMEM(part.shape, part.dtype) for part in (cells, cells, dense, *given[2:])]
+        + [dma((2, 5))],
         compiler_params=pltpu.CompilerParams(vmem_limit_bytes=60 * 1024 * 1024),
     )(*results)
     as_given = (3, 4, 0, 1, 2)

time: 47.2 us -> 45.4 us (0.962)
  Pallas kernels: 46.4 us -> 44.7 us
    pallas_call x2, Pallas kernels: 46.4 us -> 44.7 us  [the longest x1 42.9 us: body(): pl.pallas_call(functools.partial(kernel, dims), out_shape=(cells, cells,...]
where the time goes in v5:
time: 45.4 us; the launch traced here: 45.3 us
  Pallas kernels  44.7 us (98%)
  between operations  0.64 us (1%)
    pallas_call x1, Pallas kernels, body(): pl.pallas_call(functools.partial(kernel, dims), out_shape=(cells, cells,...  42.9 us
    pallas_call x1, Pallas kernels, body(): pl.pallas_call(functools.partial(store, 16 // plane), out_shape=given, in...  1.8 us

profile of v5, /device:TPU:1, one launch (start us, length us, event | category | flops | bytes accessed | tf_op | source)
XLA Modules:
  0.0 45.3 jit_solution(656889348946226539)
XLA Ops:
  0.6 42.9 %shard_map.92 = (bf16[8,4,16,128]{3,2,1,0:T(8,128)(2,1)}, bf16[8,4,16,128]{3,2,1,0:T(8,128)(2,1)}, f32[16,2,4,128]{3,2,1,0:T(4,128)}) custom-call(bf16[8,4,16,128]{3,2,1,0:T(8,128)(2,1)} %vol_in.1, bf16[3,3,3,8,32]{4,3,2,1,0:T(8,128)(2,1)} %bitcast.6, f32[1,8]{1,0:T(1,128)} %bitcast.8, bf16[3,3,3,8,32]{4,3,2,1,0:T(8,128)(2,1)} %bitcast.7, ...), custom_call_target="tpu_custom_call" | custom-call | tf_op jit(solution)/shard_map/pallas_call | solution.py:575
  43.5 1.8 %shard_map.93 = (bf16[8,4,16,128]{3,2,1,0:T(8,128)(2,1)}, bf16[8,4,16,128]{3,2,1,0:T(8,128)(2,1)}, f32[3,3,3,8,32]{4,3,2,1,0:T(8,128)}, f32[1,8]{1,0:T(1,128)}, f32[3,3,3,8,32]{4,3,2,1,0:T(8,128)}) custom-call(bf16[8,4,16,128]{3,2,1,0:T(8,128)(2,1)} %get-tuple-element.13.out_in, bf16[8,4,16,128]{3,2,1,0:T(8,128)(2,1)} %get-tuple-element.14.in_grad_in, ...), custom_call_target="tpu_custom_call" | custom-call | tf_op jit(solution)/shard_map/pallas_call | solution.py:620

commit v6 on v5

--- a/solution.py
+++ b/solution.py
@@ -109,6 +109,10 @@
     across += [{"gy": (1 - high) * n_x + col}]
     partners = across + [{"af": af_peer[k]} for k in range(1, 4)]
     partners += [{"gx": 2 * ((row + k) % n_y) + core} for k in range(1, n_y)]
+    half = col % 2
+    buddy = gy + 1 - 2 * half
+    sharers = [{"gx": 2 * row + 1 - core, "gy": gy}, {"gx": gx, "gy": buddy}, {"gx": 2 * row + 1 - core, "gy": buddy}]
+    partners.append(sharers[2])
     for dx, dy in SIDES:
         partners.append({"gx": (gx + dx + n_gx) % n_gx, "gy": ring[dy][0], "af": ring[dy][1]})
     for partner in partners:
@@ -139,22 +143,22 @@
 
     def w_copy(k):
         return pltpu.make_async_remote_copy(
-            src_ref=w_stage.at[core],
-            dst_ref=w_got.at[af, core],
+            src_ref=w_stage.at[core, half],
+            dst_ref=w_got.at[af, core, half],
             send_sem=w_send.at[k],
             recv_sem=w_recv.at[k],
             device_id={"af": af_peer[k]},
             device_id_type=MESH,
         )
 
-    def pass_copy(k):
+    def pass_copy(k, to):
         origin = (af + 4 - k) % 4
         return pltpu.make_async_remote_copy(
-            src_ref=w_got.at[origin, core],
-            dst_ref=w_got.at[origin, core],
-            send_sem=pass_send.at[k],
-            recv_sem=pass_recv.at[k],
-            device_id={"gx": 2 * row + 1 - core},
+            src_ref=w_got.at[origin, core, half],
+            dst_ref=w_got.at[origin, core, half],
+            send_sem=pass_send.at[k, to],
+            recv_sem=pass_recv.at[k, to],
+            device_id=sharers[to],
             device_id_type=MESH,
         )
 
@@ -179,8 +183,8 @@
             groups.append(jnp.concatenate(taps, axis=1))
         groups.append(jnp.zeros((8, 128), F32))
         packed = jnp.concatenate(groups, axis=0).astype(BF16)
-        w_stage[which] = packed
-        w_got[af, which] = packed
+        w_stage[which] = packed.reshape(2, 32, 128)
+        w_got[af, which] = packed.reshape(2, 32, 128)
     pl.semaphore_wait(barrier, len(partners))
     for k in (2, 1, 3):
         in_copy(VOL, k).start()
@@ -237,16 +241,18 @@
 
     for k in range(1, 4):
         w_copy(k).wait_recv()
-        pass_copy(k).start()
+        for to in (1, 2, 0):
+            pass_copy(k, to).start()
     for k in range(1, 4):
         in_copy(COT, k).wait_recv()
     assemble(COT)
     halo_start(COT)
     for k in range(1, 4):
-        pass_copy(k).wait_recv()
+        for to in range(3):
+            pass_copy(k, to).wait_recv()
 
     def taps_of(which):
-        parts = [w_got[s, which].astype(F32) for s in range(4)]
+        parts = [w_got[s, which].reshape(64, 128).astype(F32) for s in range(4)]
         groups = [
             jnp.concatenate([part[8 * a : 8 * a + 8] for part in parts], axis=0) for a in range(7)
         ]
@@ -499,7 +505,8 @@
         w_copy(k).wait_send()
         out_copy(0, k).wait_send()
         out_copy(1, k).wait_send()
-        pass_copy(k).wait_send()
+        for to in range(3):
+            pass_copy(k, to).wait_send()
     for which in (VOL, COT, HID, PRE):
         for side in SIDES:
 
@@ -587,8 +594,8 @@
             pltpu.VMEM((8, 4, 16, 128), BF16),
             pltpu.VMEM((2, 4, 4, 2, 16, 128), BF16),
             pltpu.VMEM((2, 4, 4, 2, 16, 128), BF16),
-            pltpu.VMEM((2, 64, 128), BF16),
-            pltpu.VMEM((4, 2, 64, 128), BF16),
+            pltpu.VMEM((2, 2, 32, 128), BF16),
+            pltpu.VMEM((4, 2, 2, 32, 128), BF16),
             pltpu.VMEM((4, 6, 6, 32, 128), BF16),
             pltpu.VMEM((4, 4, 32, 128), F32),
             pltpu.VMEM((4, 96, 288), BF16),
@@ -601,7 +608,7 @@
             pltpu.VMEM((16 // plane, 4, 4, 128), F32),
             pltpu.VMEM((2, 8, 16 // plane, 4, 128), F32),
             pltpu.VMEM((plane, 2 * (16 // plane), 4, 128), F32),
-            dma((2, 4)), dma((2, 4)), dma((4,)), dma((4,)), dma((4,)), dma((4,)),
+            dma((2, 4)), dma((2, 4)), dma((4,)), dma((4,)), dma((4, 3)), dma((4, 3)),
             dma((4, 8)), dma((4, 8)), dma((2, 4)), dma((2, 4)),
             dma((1,)), dma((1,)), dma((plane,)), dma((plane,)), dma((16,)), dma((16,)), dma((plane,)), dma((plane,)),
             dma((5,)), dma((3,)), pltpu.SemaphoreType.REGULAR,

time: 45.4 us -> 45.3 us (level)
  no operation moved by 1% of the time
where the time goes in v6:
time: 45.3 us; the launch traced here: 45.2 us
  Pallas kernels  44.5 us (98%)
  between operations  0.64 us (1%)
    pallas_call x1, Pallas kernels, body(): pl.pallas_call(functools.partial(kernel, dims), out_shape=(cells, cells,...  42.7 us
    pallas_call x1, Pallas kernels, body(): pl.pallas_call(functools.partial(store, 16 // plane), out_shape=given, in...  1.8 us

profile of v6, /device:TPU:1, one launch (start us, length us, event | category | flops | bytes accessed | tf_op | source)
XLA Modules:
  0.0 45.2 jit_solution(125770419108917423)
XLA Ops:
  0.6 42.7 %shard_map.92 = (bf16[8,4,16,128]{3,2,1,0:T(8,128)(2,1)}, bf16[8,4,16,128]{3,2,1,0:T(8,128)(2,1)}, f32[16,2,4,128]{3,2,1,0:T(4,128)}) custom-call(bf16[8,4,16,128]{3,2,1,0:T(8,128)(2,1)} %vol_in.1, bf16[3,3,3,8,32]{4,3,2,1,0:T(8,128)(2,1)} %bitcast.6, f32[1,8]{1,0:T(1,128)} %bitcast.8, bf16[3,3,3,8,32]{4,3,2,1,0:T(8,128)(2,1)} %bitcast.7, ...), custom_call_target="tpu_custom_call" | custom-call | tf_op jit(solution)/shard_map/pallas_call | solution.py:582
  43.4 1.8 %shard_map.93 = (bf16[8,4,16,128]{3,2,1,0:T(8,128)(2,1)}, bf16[8,4,16,128]{3,2,1,0:T(8,128)(2,1)}, f32[3,3,3,8,32]{4,3,2,1,0:T(8,128)}, f32[1,8]{1,0:T(1,128)}, f32[3,3,3,8,32]{4,3,2,1,0:T(8,128)}) custom-call(bf16[8,4,16,128]{3,2,1,0:T(8,128)(2,1)} %get-tuple-element.13.out_in, bf16[8,4,16,128]{3,2,1,0:T(8,128)(2,1)} %get-tuple-element.14.in_grad_in, ...), custom_call_target="tpu_custom_call" | custom-call | tf_op jit(solution)/shard_map/pallas_call | solution.py:627

commit v7 on v6

--- a/solution.py
+++ b/solution.py
@@ -400,11 +400,14 @@
                     rows = [lines[2 * pair + odd][8 * s : 8 * s + 8] for odd in range(2)]
                     out_stage[which, s, x, pair] = jnp.concatenate(rows, axis=0).astype(BF16)
         out_got[which, pl.ds(sub, 1)] = out_stage[which, pl.ds(af, 1)]
+
+    def send_out(which):
         for k in (2, 1, 3):
             out_copy(which, k).start()
 
     halo_wait(HID)
     produce(0, HID, 2)
+    send_out(0)
 
     pl.semaphore_wait(line_in, len(across))
     core_copy.wait_recv()
@@ -453,6 +456,7 @@
     line_others = [(k, same) for k in (4, 5, 6, 7, 2, 3, 1) for same in (1, 0)] + [(0, 0)]
     for k, same in line_others:
         line_copy(k, same).start()
+    send_out(1)
 
     def finish(which, target):
         for k in range(1, 4):

time: 45.3 us -> 45.3 us (level)
  no operation moved by 1% of the time
where the time goes in v7:
time: 45.3 us; the launch traced here: 45.2 us
  Pallas kernels  44.5 us (98%)
  between operations  0.64 us (1%)
    pallas_call x1, Pallas kernels, body(): pl.pallas_call(functools.partial(kernel, dims), out_shape=(cells, cells,...  42.7 us
    pallas_call x1, Pallas kernels, body(): pl.pallas_call(functools.partial(store, 16 // plane), out_shape=given, in...  1.8 us

profile of v7, /device:TPU:1, one launch (start us, length us, event | category | flops | bytes accessed | tf_op | source)
XLA Modules:
  0.0 45.2 jit_solution(17499661680821596221)
XLA Ops:
  0.6 42.7 %shard_map.92 = (bf16[8,4,16,128]{3,2,1,0:T(8,128)(2,1)}, bf16[8,4,16,128]{3,2,1,0:T(8,128)(2,1)}, f32[16,2,4,128]{3,2,1,0:T(4,128)}) custom-call(bf16[8,4,16,128]{3,2,1,0:T(8,128)(2,1)} %vol_in.1, bf16[3,3,3,8,32]{4,3,2,1,0:T(8,128)(2,1)} %bitcast.6, f32[1,8]{1,0:T(1,128)} %bitcast.8, bf16[3,3,3,8,32]{4,3,2,1,0:T(8,128)(2,1)} %bitcast.7, ...), custom_call_target="tpu_custom_call" | custom-call | tf_op jit(solution)/shard_map/pallas_call | solution.py:586
  43.4 1.8 %shard_map.93 = (bf16[8,4,16,128]{3,2,1,0:T(8,128)(2,1)}, bf16[8,4,16,128]{3,2,1,0:T(8,128)(2,1)}, f32[3,3,3,8,32]{4,3,2,1,0:T(8,128)}, f32[1,8]{1,0:T(1,128)}, f32[3,3,3,8,32]{4,3,2,1,0:T(8,128)}) custom-call(bf16[8,4,16,128]{3,2,1,0:T(8,128)(2,1)} %get-tuple-element.13.out_in, bf16[8,4,16,128]{3,2,1,0:T(8,128)(2,1)} %get-tuple-element.14.in_grad_in, ...), custom_call_target="tpu_custom_call" | custom-call | tf_op jit(solution)/shard_map/pallas_call | solution.py:631
